TPU v7x, 512 devices: a whole 4x8x8 slice. The times are simulated.
512 devices in a mesh: outer: 16 (over y, x_lo), inner: 32 (over z, x_hi, core).
Axes of the slice: x: 4 (x_hi: 2, x_lo: 2; x = x_hi * 2 + x_lo), y: 8, z: 8, core: 2. Of those that a mesh axis runs over, the one named last changes fastest.
Arguments:
- queries: bfloat16 [131072, 2048], P(('outer', 'inner')), may hold values from -4 to 4
- key_rows: bfloat16 [131072, 128], P(('outer', 'inner')), may hold values from -4 to 4
- value_rows: bfloat16 [131072, 128], P(('outer', 'inner')), may hold values from -6 to 6
- out_grad: bfloat16 [131072, 2048], P(('outer', 'inner')), may hold values from -96 to 96
- outputs: bfloat16 [131072, 2048], P(('outer', 'inner')), may hold values from -1.75 to 1.75
- log_sum: float32 [16, 131072], P(None, ('outer', 'inner')), may hold values from 6 to 7.5
- span_table: int32 [512, 2], replicated, may hold values from 0 to 1023, as said below
Outputs:
- query_grad: bfloat16 [131072, 2048], P(('outer', 'inner'))
- key_grad: float32 [131072, 128], P(('outer', 'inner'))
- value_grad: float32 [131072, 128], P(('outer', 'inner'))
Inputs may be any that keep to these rules, and one draw needn't show every extreme that they name: `span_table`: row e holds spans p and 1023 - p, where p over the rows is a permutation of 0 to 511.
All inputs are finite; a program needn't handle non-finite values.
Results may differ from a plain program's by a relative error of at most 0.0075.
Values may be sent and summed in bfloat16 or wider, within the bound.
No kernel may reach another device: no remote copies, remote signals or barrier semaphores. Data moves between devices by JAX's collectives and lax.ppermute only.
A program may use at most 64 MiB of HBM per device.

v0:
```python
import math

import jax
import jax.numpy as jnp
from jax import lax
from jax.sharding import PartitionSpec as P

OUT_STEPS = 2
IN_STEPS = 2


def shifted(shard, axis, by):
    devices = lax.axis_size(axis)
    return lax.ppermute(shard, axis, [(i, (i + by) % devices) for i in range(devices)])


def block_grads(
    query_block, key_block, value_block, grad_block, log_block, row_dot, query_pos, key_pos, factor
):
    scores = (
        jnp.einsum("qgd,kd->gqk", query_block, key_block, preferred_element_type=jnp.float32)
        * factor
    )
    visible = key_pos[None, None, :] <= query_pos[None, :, None]
    weights = jnp.where(visible, jnp.exp(scores - log_block[:, :, None]), 0.0)
    dweights = jnp.einsum(
        "qgd,kd->gqk", grad_block, value_block, preferred_element_type=jnp.float32
    )
    dscores = weights * (dweights - row_dot[:, :, None])
    weights_low = weights.astype(jnp.bfloat16)
    dscores_low = dscores.astype(jnp.bfloat16)
    value_part = jnp.einsum(
        "gqk,qgd->kd", weights_low, grad_block, preferred_element_type=jnp.float32
    )
    key_part = jnp.einsum(
        "gqk,qgd->kd", dscores_low, query_block, preferred_element_type=jnp.float32
    )
    query_part = jnp.einsum(
        "gqk,kd->qgd", dscores_low, key_block, preferred_element_type=jnp.float32
    )
    return (query_part, key_part, value_part)


def per_device(queries, key_rows, value_rows, out_grad, outputs, log_sum, span_table):
    head_count = log_sum.shape[0]
    head_size = key_rows.shape[1]
    row_count = key_rows.shape[0]
    span_rows = row_count // 2
    factor = 1.0 / math.sqrt(head_size)
    query_block = queries.reshape(row_count, head_count, head_size)
    grad_block = out_grad.reshape(row_count, head_count, head_size)
    row_dot = jnp.sum(
        grad_block.astype(jnp.float32)
        * outputs.reshape(row_count, head_count, head_size).astype(jnp.float32),
        axis=-1,
    ).T
    outer_count = lax.axis_size("outer")
    inner_count = lax.axis_size("inner")
    outer_index = lax.axis_index("outer")
    inner_index = lax.axis_index("inner")
    offsets = jnp.arange(span_rows, dtype=jnp.int32)

    def block_spans(a, b):
        source = (outer_index - a) % outer_count * inner_count + (inner_index - b) % inner_count
        return span_table[source]

    def positions(spans):
        return (spans[:, None] * span_rows + offsets[None, :]).reshape(row_count)

    own_spans = block_spans(0, 0)
    query_pos = positions(own_spans)
    query_total = jnp.zeros((row_count, head_count, head_size), jnp.float32)
    zero_rows = jnp.zeros((row_count, head_size), jnp.float32)
    key_total = zero_rows
    value_total = zero_rows
    group_block = (key_rows, value_rows)
    for a in range(OUT_STEPS):
        if a > 0:
            group_block = shifted((group_block[0], group_block[1]), "outer", 1)
        travel = group_block
        carried = (zero_rows, zero_rows)
        for b in range(IN_STEPS):
            if b > 0:
                travel = shifted((travel[0], travel[1]), "inner", 1)
                carried = (
                    shifted(carried[0].astype(jnp.bfloat16), "inner", 1).astype(jnp.float32),
                    shifted(carried[1].astype(jnp.bfloat16), "inner", 1).astype(jnp.float32),
                )
            key_spans = block_spans(a, b)
            query_part, key_part, value_part = block_grads(
                query_block,
                travel[0],
                travel[1],
                grad_block,
                log_sum,
                row_dot,
                query_pos,
                positions(key_spans),
                factor,
            )
            query_total = query_total + query_part
            carried = (carried[0] + key_part, carried[1] + value_part)
        carried = shifted((carried[0], carried[1]), "inner", 1 - IN_STEPS)
        if a > 0:
            carried = shifted((carried[0], carried[1]), "outer", -a)
        key_total = key_total + carried[0]
        value_total = value_total + carried[1]
    query_grad = (
        (query_total * factor).reshape(row_count, head_count * head_size).astype(jnp.bfloat16)
    )
    return (query_grad, key_total * factor, value_total)


def solution(mesh):
    placed = (
        P(("outer", "inner"), None),
        P(("outer", "inner"), None),
        P(("outer", "inner"), None),
        P(("outer", "inner"), None),
        P(("outer", "inner"), None),
        P(None, ("outer", "inner")),
        P(),
    )
    return jax.shard_map(
        per_device,
        mesh=mesh,
        in_specs=placed,
        out_specs=(
            P(("outer", "inner"), None),
            P(("outer", "inner"), None),
            P(("outer", "inner"), None),
        ),
        check_vma=False,
    )
```

profile of v0, /device:TPU:223, one launch (start us, length us, event | category | flops | bytes accessed | tf_op | source)
XLA Modules:
  0.0 96.2 jit_solution(516803359058521659)
XLA Ops:
  0.6 0.0 copy-start
  0.6 4.8 %collective-permute-start.3 = (bf16[256,128]{1,0:T(8,128)(2,1)}, bf16[256,128]{1,0:T(8,128)(2,1)S(1)}, u32[]{:S(2)}, u32[]{:S(2)}) collective-permute-start(bf16[256,128]{1,0:T(8,128)(2,1)} %param.9), channel_id=1, source_target_pairs={{0,32},{32,64},{64,96},{96,128},{128,160},{160,192},{192,224},{224... | collective-permute-start | bytes 196616 | tf_op jit(solution)/shard_map/ppermute | solution.py:14
  5.5 6.6 %collective-permute-start.1 = (bf16[256,128]{1,0:T(8,128)(2,1)}, bf16[256,128]{1,0:T(8,128)(2,1)S(1)}, u32[]{:S(2)}, u32[]{:S(2)}) collective-permute-start(bf16[256,128]{1,0:T(8,128)(2,1)} %param.9), channel_id=1, source_target_pairs={{0,1},{1,2},{2,3},{3,4},{4,5},{5,6},{6,7},{7,8},{8,9},{9,10},{10,1... | collective-permute-start | bytes 196616 | tf_op jit(solution)/shard_map/ppermute | solution.py:14
  12.1 2.5 %collective-permute-start.2 = (bf16[256,128]{1,0:T(8,128)(2,1)}, bf16[256,128]{1,0:T(8,128)(2,1)S(1)}, u32[]{:S(2)}, u32[]{:S(2)}) collective-permute-start(bf16[256,128]{1,0:T(8,128)(2,1)} %param.8), channel_id=1, source_target_pairs={{0,32},{32,64},{64,96},{96,128},{128,160},{160,192},{192,224},{224... | collective-permute-start | bytes 196616 | tf_op jit(solution)/shard_map/ppermute | solution.py:14
  14.6 2.8 %collective-permute-start = (bf16[256,128]{1,0:T(8,128)(2,1)}, bf16[256,128]{1,0:T(8,128)(2,1)S(1)}, u32[]{:S(2)}, u32[]{:S(2)}) collective-permute-start(bf16[256,128]{1,0:T(8,128)(2,1)} %param.8), channel_id=1, source_target_pairs={{0,1},{1,2},{2,3},{3,4},{4,5},{5,6},{6,7},{7,8},{8,9},{9,10},{10,1... | collective-permute-start | bytes 196616 | tf_op jit(solution)/shard_map/ppermute | solution.py:14
  17.5 1.5 %copy.75 = bf16[32,8,16,128]{3,2,1,0:T(8,128)(2,1)S(1)} copy(bf16[32,8,16,128]{3,1,2,0:T(8,128)(2,1)} %bitcast.268) | data formatting | bytes 2097152
  18.9 1.5 %convert_bitcast_fusion = f32[32,8,16,128]{3,1,2,0:T(8,128)S(1)} fusion(bf16[256,2048]{1,0:T(8,128)(2,1)} %param.11), kind=kLoop, calls=%fused_computation.28 | loop fusion | flops 524288 | bytes 3145728
  20.4 0.0 copy-start.3
  20.4 0.4 copy.76
  20.8 0.0 copy-start.4
  20.8 0.0 copy-start.2
  20.8 0.0 copy-start.5
  20.8 0.0 copy-start.6
  20.9 0.6 multiply_reduce_fusion
  21.5 0.1 copy.37
  21.6 2.7 %fusion.70 = f32[256,256,16]{1,0,2:T(8,128)} fusion(bf16[256,128]{1,0:T(8,128)(2,1)S(1)} %copy-done.3, bf16[256,2048]{1,0:T(8,128)(2,1)S(1)} %copy-done), kind=kOutput, calls=%fused_computation.69 | convolution fusion | flops 268435456 | bytes 5308416 | tf_op jit(solution)/shard_map/qgd,kd->gqk/dot_general | solution.py:21
  24.2 0.2 multiply_reduce_fusion.1
  24.5 0.1 add_bitcast_fusion
  24.5 0.1 add_bitcast_fusion.2
  24.6 0.2 broadcast_compare_fusion
  24.9 3.7 %fusion.13 = bf16[16,256,256]{1,2,0:T(8,128)(2,1)S(1)} fusion(f32[256,256,16]{1,0,2:T(8,128)} %fusion.70, f32[16,256]{1,0:T(8,128)S(1)} %copy.37, f32[16,256]{1,0:T(8,128)S(1)} %copy-done.6, pred[256,256]{0,1:T(8,128)(4,1)S(1)} %get-tuple-element.15, bf16[256,128]{1,0:T(8,128)(2,1)S(1)} %copy-done.5, bf16[256,2048]{1,0:T(8,128)(2,1)S(1)} %copy-done.2), kind=kOutput, calls=%fused_computation.20 | convolution fusion | flops 274726912 | bytes 7503872 | tf_op jit(solution)/shard_map/qgd,kd->gqk/dot_general | solution.py:26
  28.6 0.7 fusion.44
  29.3 4.5 %collective-permute-start.6 = (bf16[256,128]{1,0:T(8,128)(2,1)S(1)}, bf16[256,128]{1,0:T(8,128)(2,1)S(1)}, u32[]{:S(2)}, u32[]{:S(2)}) collective-permute-start(bf16[256,128]{1,0:T(8,128)(2,1)S(1)} %fusion.44), channel_id=1, source_target_pairs={{0,1},{1,2},{2,3},{3,4},{4,5},{5,6},{6,7},{7,8},{8,9},{9,10},{10,1... | collective-permute-start | bytes 196616 | tf_op jit(solution)/shard_map/ppermute | solution.py:14
  33.8 1.1 %fusion.49 = bf16[256,128]{1,0:T(8,128)(2,1)S(1)} fusion(f32[256,256,16]{1,0,2:T(8,128)S(1)} %copy-done.1, f32[16,256]{1,0:T(8,128)S(1)} %copy-done.6, pred[256,256]{0,1:T(8,128)(4,1)S(1)} %get-tuple-element.15, bf16[256,2048]{1,0:T(8,128)(2,1)S(1)} %copy-done.2), kind=kOutput, calls=%fused_computation.50 | convolution fusion | flops 272662528 | bytes 5390336 | tf_op jit(solution)/shard_map/gqk,qgd->kd/dot_general | solution.py:32
  34.9 0.5 fusion.100
  35.4 0.0 collective-permute-done.2
  35.4 1.9 %collective-permute-start.11 = (bf16[256,128]{1,0:T(8,128)(2,1)S(1)}, bf16[256,128]{1,0:T(8,128)(2,1)S(1)}, u32[]{:S(2)}, u32[]{:S(2)}) collective-permute-start(bf16[256,128]{1,0:T(8,128)(2,1)S(1)} %fusion.49), channel_id=1, source_target_pairs={{0,1},{1,2},{2,3},{3,4},{4,5},{5,6},{6,7},{7,8},{8,9},{9,10},{10,1... | collective-permute-start | bytes 196616 | tf_op jit(solution)/shard_map/ppermute | solution.py:14
  37.3 0.7 fusion.66
  38.0 1.1 %fusion.46 = bf16[256,128]{1,0:T(8,128)(2,1)S(1)} fusion(f32[256,256,16]{1,0,2:T(8,128)S(1)} %fusion.66, f32[16,256]{1,0:T(8,128)S(1)} %copy-done.6, pred[256,256]{0,1:T(8,128)(4,1)S(1)} %get-tuple-element.14, bf16[256,2048]{1,0:T(8,128)(2,1)S(1)} %copy-done.2), kind=kOutput, calls=%fused_computation.49 | convolution fusion | flops 272662528 | bytes 5390336 | tf_op jit(solution)/shard_map/gqk,qgd->kd/dot_general | solution.py:32
  39.1 0.0 collective-permute-done.3
  39.1 1.5 %fusion.5 = bf16[16,256,256]{1,2,0:T(8,128)(2,1)S(1)} fusion(f32[256,256,16]{1,0,2:T(8,128)S(1)} %fusion.66, f32[16,256]{1,0:T(8,128)S(1)} %copy.37, f32[16,256]{1,0:T(8,128)S(1)} %copy-done.6, pred[256,256]{0,1:T(8,128)(4,1)S(1)} %get-tuple-element.14, bf16[256,128]{1,0:T(8,128)(2,1)S(1)} %collective-permute-done.3, bf16[256,2048]{1,0:T(8,128)(2,1)S(1)} %copy-done.2), kind=kOutput, calls=%fused_computation.8 | convolution fusion | flops 274726912 | bytes 7503872 | tf_op jit(solution)/shard_map/qgd,kd->gqk/dot_general | solution.py:26
  40.6 0.7 fusion.45
  41.3 3.1 %collective-permute-start.8 = (bf16[256,128]{1,0:T(8,128)(2,1)S(1)}, bf16[256,128]{1,0:T(8,128)(2,1)S(1)}, u32[]{:S(2)}, u32[]{:S(2)}) collective-permute-start(bf16[256,128]{1,0:T(8,128)(2,1)S(1)} %fusion.45), channel_id=1, source_target_pairs={{0,1},{1,2},{2,3},{3,4},{4,5},{5,6},{6,7},{7,8},{8,9},{9,10},{10,1... | collective-permute-start | bytes 196616 | tf_op jit(solution)/shard_map/ppermute | solution.py:14
  44.5 2.8 %collective-permute-start.13 = (bf16[256,128]{1,0:T(8,128)(2,1)S(1)}, bf16[256,128]{1,0:T(8,128)(2,1)S(1)}, u32[]{:S(2)}, u32[]{:S(2)}) collective-permute-start(bf16[256,128]{1,0:T(8,128)(2,1)S(1)} %fusion.46), channel_id=1, source_target_pairs={{0,1},{1,2},{2,3},{3,4},{4,5},{5,6},{6,7},{7,8},{8,9},{9,10},{10,1... | collective-permute-start | bytes 196616 | tf_op jit(solution)/shard_map/ppermute | solution.py:14
  47.3 0.7 fusion.68
  48.0 1.1 %convert_add_fusion.1 = f32[256,128]{1,0:T(8,128)S(1)} fusion(bf16[256,128]{1,0:T(8,128)(2,1)S(1)} %collective-permute-done.11, f32[256,256,16]{1,0,2:T(8,128)S(1)} %fusion.68, f32[16,256]{1,0:T(8,128)S(1)} %copy-done.6, pred[256,256]{0,1:T(8,128)(4,1)S(1)} %get-tuple-element.16, bf16[256,2048]{1,0:T(8,128)(2,1)S(1)} %copy-done.2), kind=kOutput, calls=%fused_computation.88 | convolution fusion | flops 272695296 | bytes 5521408 | tf_op jit(solution)/shard_map/gqk,qgd->kd/dot_general | solution.py:32
  49.1 2.1 %collective-permute-start.12 = (f32[256,128]{1,0:T(8,128)S(1)}, f32[256,128]{1,0:T(8,128)S(1)}, u32[]{:S(2)}, u32[]{:S(2)}) collective-permute-start(f32[256,128]{1,0:T(8,128)S(1)} %convert_add_fusion.1), channel_id=1, source_target_pairs={{0,31},{1,0},{2,1},{3,2},{4,3},{5,4},{6,5},{7,6},{8,7},{9,8},{10,9... | collective-permute-start | bytes 393224 | tf_op jit(solution)/shard_map/ppermute | solution.py:14
  51.2 0.0 collective-permute-done.1
  51.2 1.5 %fusion.9 = bf16[16,256,256]{1,2,0:T(8,128)(2,1)S(1)} fusion(f32[256,256,16]{1,0,2:T(8,128)S(1)} %fusion.68, f32[16,256]{1,0:T(8,128)S(1)} %copy.37, f32[16,256]{1,0:T(8,128)S(1)} %copy-done.6, pred[256,256]{0,1:T(8,128)(4,1)S(1)} %get-tuple-element.16, bf16[256,128]{1,0:T(8,128)(2,1)S(1)} %collective-permute-done.1, bf16[256,2048]{1,0:T(8,128)(2,1)S(1)} %copy-done.2), kind=kOutput, calls=%fused_computation.14 | convolution fusion | flops 274726912 | bytes 7503872 | tf_op jit(solution)/shard_map/qgd,kd->gqk/dot_general | solution.py:26
  52.7 0.7 convert_add_fusion.3
  53.4 3.5 %collective-permute-start.7 = (f32[256,128]{1,0:T(8,128)S(1)}, f32[256,128]{1,0:T(8,128)S(1)}, u32[]{:S(2)}, u32[]{:S(2)}) collective-permute-start(f32[256,128]{1,0:T(8,128)S(1)} %convert_add_fusion.3), channel_id=1, source_target_pairs={{0,31},{1,0},{2,1},{3,2},{4,3},{5,4},{6,5},{7,6},{8,7},{9,8},{10,9... | collective-permute-start | bytes 393224 | tf_op jit(solution)/shard_map/ppermute | solution.py:14
  57.0 5.6 %collective-permute-start.4 = (bf16[256,128]{1,0:T(8,128)(2,1)S(1)}, bf16[256,128]{1,0:T(8,128)(2,1)S(1)}, u32[]{:S(2)}, u32[]{:S(2)}) collective-permute-start(bf16[256,128]{1,0:T(8,128)(2,1)S(1)} %collective-permute-done.2), channel_id=1, source_target_pairs={{0,1},{1,2},{2,3},{3,4},{4,5},{5,6},{6,7},{7,8},{8,9},{9,10},{10,1... | collective-permute-start | bytes 196616 | tf_op jit(solution)/shard_map/ppermute | solution.py:14
  62.6 0.5 fusion.96
  63.1 0.8 collective-permute-done.4
  63.9 7.9 %collective-permute-start.5 = (bf16[256,128]{1,0:T(8,128)(2,1)S(1)}, bf16[256,128]{1,0:T(8,128)(2,1)S(1)}, u32[]{:S(2)}, u32[]{:S(2)}) collective-permute-start(bf16[256,128]{1,0:T(8,128)(2,1)S(1)} %collective-permute-done.3), channel_id=1, source_target_pairs={{0,1},{1,2},{2,3},{3,4},{4,5},{5,6},{6,7},{7,8},{8,9},{9,10},{10,1... | collective-permute-start | bytes 196616 | tf_op jit(solution)/shard_map/ppermute | solution.py:14
  71.8 0.7 fusion.64
  72.5 0.0 collective-permute-done.13
  72.5 1.1 %convert_add_fusion = f32[256,128]{1,0:T(8,128)S(1)} fusion(bf16[256,128]{1,0:T(8,128)(2,1)S(1)} %collective-permute-done.13, f32[256,256,16]{1,0,2:T(8,128)S(1)} %fusion.64, f32[16,256]{1,0:T(8,128)S(1)} %copy-done.6, pred[256,256]{0,1:T(8,128)(4,1)S(1)} %get-tuple-element.13, bf16[256,2048]{1,0:T(8,128)(2,1)S(1)} %copy-done.2), kind=kOutput, calls=%fused_computation.87 | convolution fusion | flops 272695296 | bytes 5521408 | tf_op jit(solution)/shard_map/gqk,qgd->kd/dot_general | solution.py:32
  73.6 1.9 %collective-permute-start.14 = (f32[256,128]{1,0:T(8,128)S(1)}, f32[256,128]{1,0:T(8,128)S(1)}, u32[]{:S(2)}, u32[]{:S(2)}) collective-permute-start(f32[256,128]{1,0:T(8,128)S(1)} %convert_add_fusion), channel_id=1, source_target_pairs={{0,31},{1,0},{2,1},{3,2},{4,3},{5,4},{6,5},{7,6},{8,7},{9,8},{10,9... | collective-permute-start | bytes 393224 | tf_op jit(solution)/shard_map/ppermute | solution.py:14
  75.5 0.0 collective-permute-done.5
  75.5 1.5 %fusion.1 = bf16[16,256,256]{1,2,0:T(8,128)(2,1)S(1)} fusion(f32[256,256,16]{1,0,2:T(8,128)S(1)} %fusion.64, f32[16,256]{1,0:T(8,128)S(1)} %copy.37, f32[16,256]{1,0:T(8,128)S(1)} %copy-done.6, pred[256,256]{0,1:T(8,128)(4,1)S(1)} %get-tuple-element.13, bf16[256,128]{1,0:T(8,128)(2,1)S(1)} %collective-permute-done.5, bf16[256,2048]{1,0:T(8,128)(2,1)S(1)} %copy-done.2), kind=kOutput, calls=%fused_computation.2 | convolution fusion | flops 274726912 | bytes 7503872 | tf_op jit(solution)/shard_map/qgd,kd->gqk/dot_general | solution.py:26
  77.0 0.7 convert_add_fusion.2
  77.7 1.9 %collective-permute-start.9 = (f32[256,128]{1,0:T(8,128)S(1)}, f32[256,128]{1,0:T(8,128)S(1)}, u32[]{:S(2)}, u32[]{:S(2)}) collective-permute-start(f32[256,128]{1,0:T(8,128)S(1)} %convert_add_fusion.2), channel_id=1, source_target_pairs={{0,31},{1,0},{2,1},{3,2},{4,3},{5,4},{6,5},{7,6},{8,7},{9,8},{10,9... | collective-permute-start | bytes 393224 | tf_op jit(solution)/shard_map/ppermute | solution.py:14
  79.7 0.5 fusion.92
  80.2 3.3 %collective-permute-done.14 = f32[256,128]{1,0:T(8,128)S(1)} collective-permute-done((f32[256,128]{1,0:T(8,128)S(1)}, f32[256,128]{1,0:T(8,128)S(1)}, u32[]{:S(2)}, u32[]{:S(2)}) %collective-permute-start.14) | collective-permute-done | bytes 131104 | tf_op jit(solution)/shard_map/ppermute | solution.py:14
  83.5 2.3 %collective-permute-start.15 = (f32[256,128]{1,0:T(8,128)S(1)}, f32[256,128]{1,0:T(8,128)S(1)}, u32[]{:S(2)}, u32[]{:S(2)}) collective-permute-start(f32[256,128]{1,0:T(8,128)S(1)} %collective-permute-done.14), channel_id=1, source_target_pairs={{0,480},{32,0},{64,32},{96,64},{128,96},{160,128},{192,160},{224,1... | collective-permute-start | bytes 393224 | tf_op jit(solution)/shard_map/ppermute | solution.py:14
  85.8 1.9 %collective-permute-done.9 = f32[256,128]{1,0:T(8,128)S(1)} collective-permute-done((f32[256,128]{1,0:T(8,128)S(1)}, f32[256,128]{1,0:T(8,128)S(1)}, u32[]{:S(2)}, u32[]{:S(2)}) %collective-permute-start.9) | collective-permute-done | bytes 131104 | tf_op jit(solution)/shard_map/ppermute | solution.py:14
  87.8 3.4 %collective-permute-start.10 = (f32[256,128]{1,0:T(8,128)S(1)}, f32[256,128]{1,0:T(8,128)S(1)}, u32[]{:S(2)}, u32[]{:S(2)}) collective-permute-start(f32[256,128]{1,0:T(8,128)S(1)} %collective-permute-done.9), channel_id=1, source_target_pairs={{0,480},{32,0},{64,32},{96,64},{128,96},{160,128},{192,160},{224,1... | collective-permute-start | bytes 393224 | tf_op jit(solution)/shard_map/ppermute | solution.py:14
  91.2 1.0 %multiply_convert_fusion = bf16[16,256,128]{1,2,0:T(8,128)(2,1)S(1)} fusion(f32[16,256,128]{1,2,0:T(8,128)S(1)} %fusion.92, f32[16,256,128]{1,2,0:T(8,128)S(1)} %fusion.100, f32[16,256,128]{1,2,0:T(8,128)S(1)} %fusion.96, bf16[16,256,256]{1,2,0:T(8,128)(2,1)S(1)} %fusion.1, bf16[256,128]{1,0:T(8,128)(2,1)S(1)} %collective-permute-done.4), kind=kOutput, calls=%fused_computation.29 | convolution fusion | flops 271056896 | bytes 9502720 | tf_op jit(solution)/shard_map/gqk,kd->qgd/dot_general | solution.py:38
  92.2 1.4 %copy.60 = bf16[256,2048]{1,0:T(8,128)(2,1)} copy(bf16[256,2048]{0,1:T(8,128)(2,1)S(1)} %bitcast.266) | data formatting | bytes 2097152
  93.6 0.0 collective-permute-done.12
  93.6 0.7 add.204
  94.3 1.3 %collective-permute-done.10 = f32[256,128]{1,0:T(8,128)S(1)} collective-permute-done((f32[256,128]{1,0:T(8,128)S(1)}, f32[256,128]{1,0:T(8,128)S(1)}, u32[]{:S(2)}, u32[]{:S(2)}) %collective-permute-start.10) | collective-permute-done | bytes 131104 | tf_op jit(solution)/shard_map/ppermute | solution.py:14
  95.6 0.7 add_multiply_fusion
  (14 shorter events, 0.0 us)
Async XLA Ops:
  0.6 20.9 %copy-start = (bf16[256,2048]{1,0:T(8,128)(2,1)S(1)}, bf16[256,2048]{1,0:T(8,128)(2,1)}, u32[]{:S(2)}) copy-start(bf16[256,2048]{1,0:T(8,128)(2,1)} %param.7) | copy-start | bytes 3145732
  0.6 38.5 %collective-permute-start.3 = (bf16[256,128]{1,0:T(8,128)(2,1)}, bf16[256,128]{1,0:T(8,128)(2,1)S(1)}, u32[]{:S(2)}, u32[]{:S(2)}) collective-permute-start(bf16[256,128]{1,0:T(8,128)(2,1)} %param.9), channel_id=1, source_target_pairs={{0,32},{32,64},{64,96},{96,128},{128,160},{160,192},{192,224},{224... | collective-permute-start | bytes 196616 | tf_op jit(solution)/shard_map/ppermute | solution.py:14
  5.5 45.7 %collective-permute-start.1 = (bf16[256,128]{1,0:T(8,128)(2,1)}, bf16[256,128]{1,0:T(8,128)(2,1)S(1)}, u32[]{:S(2)}, u32[]{:S(2)}) collective-permute-start(bf16[256,128]{1,0:T(8,128)(2,1)} %param.9), channel_id=1, source_target_pairs={{0,1},{1,2},{2,3},{3,4},{4,5},{5,6},{6,7},{7,8},{8,9},{9,10},{10,1... | collective-permute-start | bytes 196616 | tf_op jit(solution)/shard_map/ppermute | solution.py:14
  12.1 23.3 %collective-permute-start.2 = (bf16[256,128]{1,0:T(8,128)(2,1)}, bf16[256,128]{1,0:T(8,128)(2,1)S(1)}, u32[]{:S(2)}, u32[]{:S(2)}) collective-permute-start(bf16[256,128]{1,0:T(8,128)(2,1)} %param.8), channel_id=1, source_target_pairs={{0,32},{32,64},{64,96},{96,128},{128,160},{160,192},{192,224},{224... | collective-permute-start | bytes 196616 | tf_op jit(solution)/shard_map/ppermute | solution.py:14
  14.6 29.9 %collective-permute-start = (bf16[256,128]{1,0:T(8,128)(2,1)}, bf16[256,128]{1,0:T(8,128)(2,1)S(1)}, u32[]{:S(2)}, u32[]{:S(2)}) collective-permute-start(bf16[256,128]{1,0:T(8,128)(2,1)} %param.8), channel_id=1, source_target_pairs={{0,1},{1,2},{2,3},{3,4},{4,5},{5,6},{6,7},{7,8},{8,9},{9,10},{10,1... | collective-permute-start | bytes 196616 | tf_op jit(solution)/shard_map/ppermute | solution.py:14
  20.4 1.1 %copy-start.3 = (bf16[256,128]{1,0:T(8,128)(2,1)S(1)}, bf16[256,128]{1,0:T(8,128)(2,1)}, u32[]{:S(2)}) copy-start(bf16[256,128]{1,0:T(8,128)(2,1)} %param.8) | copy-start | bytes 196612
  20.8 3.4 %copy-start.4 = (s32[512,2]{0,1:T(2,128)S(1)}, s32[512,2]{0,1:T(2,128)}, u32[]{:S(2)}) copy-start(s32[512,2]{0,1:T(2,128)} %param.13) | copy-start | bytes 12292
  20.8 4.0 %copy-start.2 = (bf16[256,2048]{1,0:T(8,128)(2,1)S(1)}, bf16[256,2048]{1,0:T(8,128)(2,1)}, u32[]{:S(2)}) copy-start(bf16[256,2048]{1,0:T(8,128)(2,1)} %param.10) | copy-start | bytes 3145732
  20.8 4.0 %copy-start.5 = (bf16[256,128]{1,0:T(8,128)(2,1)S(1)}, bf16[256,128]{1,0:T(8,128)(2,1)}, u32[]{:S(2)}) copy-start(bf16[256,128]{1,0:T(8,128)(2,1)} %param.9) | copy-start | bytes 196612
  20.8 4.0 %copy-start.6 = (f32[16,256]{1,0:T(8,128)S(1)}, f32[16,256]{1,0:T(8,128)}, u32[]{:S(2)}) copy-start(f32[16,256]{1,0:T(8,128)} %param.12) | copy-start | bytes 49156
  24.9 8.9 %copy-start.1 = (f32[256,256,16]{1,0,2:T(8,128)S(1)}, f32[256,256,16]{1,0,2:T(8,128)}, u32[]{:S(2)}) copy-start(f32[256,256,16]{1,0,2:T(8,128)} %fusion.70) | copy-start | bytes 12582916
  29.3 23.3 %collective-permute-start.6 = (bf16[256,128]{1,0:T(8,128)(2,1)S(1)}, bf16[256,128]{1,0:T(8,128)(2,1)S(1)}, u32[]{:S(2)}, u32[]{:S(2)}) collective-permute-start(bf16[256,128]{1,0:T(8,128)(2,1)S(1)} %fusion.44), channel_id=1, source_target_pairs={{0,1},{1,2},{2,3},{3,4},{4,5},{5,6},{6,7},{7,8},{8,9},{9,10},{10,1... | collective-permute-start | bytes 196616 | tf_op jit(solution)/shard_map/ppermute | solution.py:14
  35.4 12.6 %collective-permute-start.11 = (bf16[256,128]{1,0:T(8,128)(2,1)S(1)}, bf16[256,128]{1,0:T(8,128)(2,1)S(1)}, u32[]{:S(2)}, u32[]{:S(2)}) collective-permute-start(bf16[256,128]{1,0:T(8,128)(2,1)S(1)} %fusion.49), channel_id=1, source_target_pairs={{0,1},{1,2},{2,3},{3,4},{4,5},{5,6},{6,7},{7,8},{8,9},{9,10},{10,1... | collective-permute-start | bytes 196616 | tf_op jit(solution)/shard_map/ppermute | solution.py:14
  41.3 35.7 %collective-permute-start.8 = (bf16[256,128]{1,0:T(8,128)(2,1)S(1)}, bf16[256,128]{1,0:T(8,128)(2,1)S(1)}, u32[]{:S(2)}, u32[]{:S(2)}) collective-permute-start(bf16[256,128]{1,0:T(8,128)(2,1)S(1)} %fusion.45), channel_id=1, source_target_pairs={{0,1},{1,2},{2,3},{3,4},{4,5},{5,6},{6,7},{7,8},{8,9},{9,10},{10,1... | collective-permute-start | bytes 196616 | tf_op jit(solution)/shard_map/ppermute | solution.py:14
  44.5 28.0 %collective-permute-start.13 = (bf16[256,128]{1,0:T(8,128)(2,1)S(1)}, bf16[256,128]{1,0:T(8,128)(2,1)S(1)}, u32[]{:S(2)}, u32[]{:S(2)}) collective-permute-start(bf16[256,128]{1,0:T(8,128)(2,1)S(1)} %fusion.46), channel_id=1, source_target_pairs={{0,1},{1,2},{2,3},{3,4},{4,5},{5,6},{6,7},{7,8},{8,9},{9,10},{10,1... | collective-permute-start | bytes 196616 | tf_op jit(solution)/shard_map/ppermute | solution.py:14
  49.1 44.5 %collective-permute-start.12 = (f32[256,128]{1,0:T(8,128)S(1)}, f32[256,128]{1,0:T(8,128)S(1)}, u32[]{:S(2)}, u32[]{:S(2)}) collective-permute-start(f32[256,128]{1,0:T(8,128)S(1)} %convert_add_fusion.1), channel_id=1, source_target_pairs={{0,31},{1,0},{2,1},{3,2},{4,3},{5,4},{6,5},{7,6},{8,7},{9,8},{10,9... | collective-permute-start | bytes 393224 | tf_op jit(solution)/shard_map/ppermute | solution.py:14
  53.4 40.9 %collective-permute-start.7 = (f32[256,128]{1,0:T(8,128)S(1)}, f32[256,128]{1,0:T(8,128)S(1)}, u32[]{:S(2)}, u32[]{:S(2)}) collective-permute-start(f32[256,128]{1,0:T(8,128)S(1)} %convert_add_fusion.3), channel_id=1, source_target_pairs={{0,31},{1,0},{2,1},{3,2},{4,3},{5,4},{6,5},{7,6},{8,7},{9,8},{10,9... | collective-permute-start | bytes 393224 | tf_op jit(solution)/shard_map/ppermute | solution.py:14
  57.0 6.9 %collective-permute-start.4 = (bf16[256,128]{1,0:T(8,128)(2,1)S(1)}, bf16[256,128]{1,0:T(8,128)(2,1)S(1)}, u32[]{:S(2)}, u32[]{:S(2)}) collective-permute-start(bf16[256,128]{1,0:T(8,128)(2,1)S(1)} %collective-permute-done.2), channel_id=1, source_target_pairs={{0,1},{1,2},{2,3},{3,4},{4,5},{5,6},{6,7},{7,8},{8,9},{9,10},{10,1... | collective-permute-start | bytes 196616 | tf_op jit(solution)/shard_map/ppermute | solution.py:14
  63.9 11.6 %collective-permute-start.5 = (bf16[256,128]{1,0:T(8,128)(2,1)S(1)}, bf16[256,128]{1,0:T(8,128)(2,1)S(1)}, u32[]{:S(2)}, u32[]{:S(2)}) collective-permute-start(bf16[256,128]{1,0:T(8,128)(2,1)S(1)} %collective-permute-done.3), channel_id=1, source_target_pairs={{0,1},{1,2},{2,3},{3,4},{4,5},{5,6},{6,7},{7,8},{8,9},{9,10},{10,1... | collective-permute-start | bytes 196616 | tf_op jit(solution)/shard_map/ppermute | solution.py:14
  73.6 9.9 %collective-permute-start.14 = (f32[256,128]{1,0:T(8,128)S(1)}, f32[256,128]{1,0:T(8,128)S(1)}, u32[]{:S(2)}, u32[]{:S(2)}) collective-permute-start(f32[256,128]{1,0:T(8,128)S(1)} %convert_add_fusion), channel_id=1, source_target_pairs={{0,31},{1,0},{2,1},{3,2},{4,3},{5,4},{6,5},{7,6},{8,7},{9,8},{10,9... | collective-permute-start | bytes 393224 | tf_op jit(solution)/shard_map/ppermute | solution.py:14
  77.7 10.0 %collective-permute-start.9 = (f32[256,128]{1,0:T(8,128)S(1)}, f32[256,128]{1,0:T(8,128)S(1)}, u32[]{:S(2)}, u32[]{:S(2)}) collective-permute-start(f32[256,128]{1,0:T(8,128)S(1)} %convert_add_fusion.2), channel_id=1, source_target_pairs={{0,31},{1,0},{2,1},{3,2},{4,3},{5,4},{6,5},{7,6},{8,7},{9,8},{10,9... | collective-permute-start | bytes 393224 | tf_op jit(solution)/shard_map/ppermute | solution.py:14
  83.5 10.1 %collective-permute-start.15 = (f32[256,128]{1,0:T(8,128)S(1)}, f32[256,128]{1,0:T(8,128)S(1)}, u32[]{:S(2)}, u32[]{:S(2)}) collective-permute-start(f32[256,128]{1,0:T(8,128)S(1)} %collective-permute-done.14), channel_id=1, source_target_pairs={{0,480},{32,0},{64,32},{96,64},{128,96},{160,128},{192,160},{224,1... | collective-permute-start | bytes 393224 | tf_op jit(solution)/shard_map/ppermute | solution.py:14
  87.8 7.8 %collective-permute-start.10 = (f32[256,128]{1,0:T(8,128)S(1)}, f32[256,128]{1,0:T(8,128)S(1)}, u32[]{:S(2)}, u32[]{:S(2)}) collective-permute-start(f32[256,128]{1,0:T(8,128)S(1)} %collective-permute-done.9), channel_id=1, source_target_pairs={{0,480},{32,0},{64,32},{96,64},{128,96},{160,128},{192,160},{224,1... | collective-permute-start | bytes 393224 | tf_op jit(solution)/shard_map/ppermute | solution.py:14
where the time goes:
time: 96.9 us; the launch traced here: 96.2 us
  starting transfers between devices  57.8 us (60%)
  matrix products  22.5 us (23%)
  waiting for transfers between devices  7.38 us (8%)
  other arithmetic  4 us (4%)
  local copies, waits for them, and re-layouts  3.37 us (3%)
  between operations  1.13 us (1%)
    ppermute x16, starting transfers between devices, shifted(): lax.ppermute(shard, axis, [(i, (i + by) % devices) for i in range(devices)])  57.8 us
    dot_general x4, matrix products, block_grads(): jnp.einsum('qgd,kd->gqk', grad_block, value_block, preferred_element_type...  8.14 us
    ppermute x16, waiting for transfers between devices, shifted(): lax.ppermute(shard, axis, [(i, (i + by) % devices) for i in range(devices)])  7.38 us
    dot_general x4, matrix products, block_grads(): jnp.einsum('qgd,kd->gqk', query_block, key_block, preferred_element_type=...  4.81 us
    dot_general x4, matrix products, block_grads(): jnp.einsum('gqk,qgd->kd', weights_low, grad_block, preferred_element_type...  4.27 us
    unnamed x17, local copies, waits for them, and re-layouts  3.31 us
    dot_general x4, matrix products, block_grads(): jnp.einsum('gqk,qgd->kd', dscores_low, query_block, preferred_element_typ...  2.89 us
    dot_general x4, matrix products, block_grads(): jnp.einsum('gqk,kd->qgd', dscores_low, key_block, preferred_element_type=...  2.43 us
  transfers between devices with their start and end apart: 16, of which 4 were waited for; matrix products, arithmetic and copies ran while one was open for 30% of the time, Pallas kernels for 0%

commit v1 on v0

v1 whole, which is shorter than its diff:
```python
import functools
import math

import jax
import jax.numpy as jnp
from jax import lax
from jax.experimental import pallas as pl
from jax.experimental.pallas import tpu as pltpu
from jax.sharding import PartitionSpec as P

F32 = jnp.float32
BF16 = jnp.bfloat16
HEADS = 16
HD = 128
SPAN = 128
WIDE = HEADS * HD
FACTOR = 1.0 / math.sqrt(HD)
LOG2E = math.log2(math.e)


def dot(a, b, contract):
    return lax.dot_general(a, b, ((contract[:1], contract[1:]), ((), ())), preferred_element_type=F32)


def heads_of(ref, rows):
    return [ref[rows, h * HD : (h + 1) * HD] for h in range(HEADS)]


def sub_block(key, value, queries, grads, log_two, row_dot, mask=None):
    probs, dscores = [], []
    for m in range(0, HEADS, 2):
        pair = jnp.concatenate(queries[m : m + 2], 0)
        grad = jnp.concatenate(grads[m : m + 2], 0)
        lanes = lambda x: jnp.concatenate([x[m : m + 1], x[m + 1 : m + 2]], 1)
        scores = dot(key, pair, (1, 1))
        weights = jnp.exp2(scores * (FACTOR * LOG2E) - lanes(log_two))
        if mask is not None:
            weights = jnp.where(mask, weights, 0.0)
        dweights = dot(value, grad, (1, 1))
        probs.append(weights.astype(BF16))
        dscores.append((weights * (dweights - lanes(row_dot))).astype(BF16))
    return jnp.concatenate(probs, 1), jnp.concatenate(dscores, 1)


def prep_kernel(grad_ref, out_ref, log_ref, log_two_ref, row_dot_ref):
    log_two_ref[...] = log_ref[...] * LOG2E
    columns = []
    for h in range(HEADS):
        one = slice(h * HD, (h + 1) * HD)
        product = grad_ref[:, one].astype(F32) * out_ref[:, one].astype(F32)
        columns.append(jnp.sum(product, axis=1, keepdims=True))
    row_dot_ref[...] = jnp.concatenate(columns, 1).T


def remote_kernel(half_ref, query_ref, grad_ref, kv_ref, log_ref, dot_ref, part_ref, first_ref, second_ref):
    half = half_ref[0]
    rows = pl.ds(pl.multiple_of(half * SPAN, SPAN), SPAN)
    high = slice(SPAN, 2 * SPAN)
    query_high, grad_high = heads_of(query_ref, high), heads_of(grad_ref, high)
    probs, dscores = sub_block(
        kv_ref[0:SPAN, :], kv_ref[2 * SPAN : 3 * SPAN, :], query_high, grad_high, log_ref[:, high], dot_ref[:, high]
    )
    first_ref[...] = dscores
    key_low = dot(dscores, jnp.concatenate(query_high, 0), (1, 0))
    value_low = dot(probs, jnp.concatenate(grad_high, 0), (1, 0))
    query_half, grad_half = heads_of(query_ref, rows), heads_of(grad_ref, rows)
    is_low = half == 0
    probs, dscores = sub_block(
        kv_ref[rows, :],
        kv_ref[pl.ds(pl.multiple_of((half + 2) * SPAN, SPAN), SPAN), :],
        query_half,
        grad_half,
        jnp.where(is_low, log_ref[:, 0:SPAN], log_ref[:, high]),
        jnp.where(is_low, dot_ref[:, 0:SPAN], dot_ref[:, high]),
    )
    second_ref[...] = dscores
    key_half = dot(dscores, jnp.concatenate(query_half, 0), (1, 0))
    value_half = dot(probs, jnp.concatenate(grad_half, 0), (1, 0))
    part_ref[0:SPAN, :] = (key_low + jnp.where(is_low, key_half, 0.0)).astype(BF16)
    part_ref[SPAN : 2 * SPAN, :] = jnp.where(is_low, 0.0, key_half).astype(BF16)
    part_ref[2 * SPAN : 3 * SPAN, :] = (value_low + jnp.where(is_low, value_half, 0.0)).astype(BF16)
    part_ref[3 * SPAN :, :] = jnp.where(is_low, 0.0, value_half).astype(BF16)


def own_kernel(
    half_ref,
    query_ref,
    grad_ref,
    kv_ref,
    log_ref,
    dot_ref,
    kv1_ref,
    kv2_ref,
    kv3_ref,
    first1_ref,
    second1_ref,
    first2_ref,
    second2_ref,
    first3_ref,
    second3_ref,
    query_grad_ref,
    key_grad_ref,
    value_grad_ref,
):
    low, high = slice(0, SPAN), slice(SPAN, 2 * SPAN)
    span = (SPAN, 2 * SPAN)
    keys = lax.broadcasted_iota(jnp.int32, span, 0)
    mask = keys <= lax.rem(lax.broadcasted_iota(jnp.int32, span, 1), SPAN)
    query_low, grad_low = heads_of(query_ref, low), heads_of(grad_ref, low)
    query_high, grad_high = heads_of(query_ref, high), heads_of(grad_ref, high)
    key_low, key_high = kv_ref[low, :], kv_ref[high, :]
    value_low, value_high = kv_ref[2 * SPAN : 3 * SPAN, :], kv_ref[3 * SPAN :, :]
    log_low, log_high, dot_low, dot_high = log_ref[:, low], log_ref[:, high], dot_ref[:, low], dot_ref[:, high]
    probs_ll, ds_ll = sub_block(key_low, value_low, query_low, grad_low, log_low, dot_low, mask)
    probs_lh, ds_lh = sub_block(key_low, value_low, query_high, grad_high, log_high, dot_high)
    probs_hh, ds_hh = sub_block(key_high, value_high, query_high, grad_high, log_high, dot_high, mask)
    all_low, all_high = jnp.concatenate(query_low, 0), jnp.concatenate(query_high, 0)
    key_grad_ref[low, :] = dot(ds_ll, all_low, (1, 0)) + dot(ds_lh, all_high, (1, 0))
    key_grad_ref[high, :] = dot(ds_hh, all_high, (1, 0))
    all_low, all_high = jnp.concatenate(grad_low, 0), jnp.concatenate(grad_high, 0)
    value_grad_ref[low, :] = dot(probs_ll, all_low, (1, 0)) + dot(probs_lh, all_high, (1, 0))
    value_grad_ref[high, :] = dot(probs_hh, all_high, (1, 0))

    zero = jnp.zeros((SPAN, HD), BF16)
    low_keys, low_scores = [key_low], [ds_ll]
    high_keys, high_scores = [key_low, key_high], [ds_lh, ds_hh]
    remotes = ((kv1_ref, first1_ref, second1_ref), (kv2_ref, first2_ref, second2_ref), (kv3_ref, first3_ref, second3_ref))
    for j, (ref, first, second) in enumerate(remotes):
        is_low = half_ref[j] == 0
        high_keys += [ref[low, :], jnp.where(is_low, zero, ref[high, :])]
        high_scores += [first[...], second[...]]
        low_keys.append(jnp.where(is_low, ref[low, :], zero))
        low_scores.append(second[...])
    for rows, key_list, score_list in ((low, low_keys, low_scores), (high, high_keys, high_scores)):
        total = dot(jnp.concatenate(key_list, 0).T, jnp.concatenate(score_list, 0), (1, 0)) * FACTOR
        for h in range(HEADS):
            one = slice(h * HD, (h + 1) * HD)
            query_grad_ref[rows, one] = total[:, one].T.astype(BF16)


VMEM = pl.BlockSpec(memory_space=pltpu.VMEM)
SMEM = pl.BlockSpec(memory_space=pltpu.SMEM)
PARAMS = pltpu.CompilerParams(vmem_limit_bytes=24 << 20)


def units(count):
    return pl.CostEstimate(flops=count * 10 * SPAN * HD * SPAN * HEADS, bytes_accessed=1 << 20, transcendentals=count * SPAN * SPAN * HEADS)


def shifted(shard, by_outer, by_inner):
    outer, inner = lax.axis_size("outer"), lax.axis_size("inner")
    pairs = [
        (o * inner + i, (o + by_outer) % outer * inner + (i + by_inner) % inner) for o in range(outer) for i in range(inner)
    ]
    return lax.ppermute(shard, ("outer", "inner"), pairs)


def per_device(queries, key_rows, value_rows, out_grad, outputs, log_sum, span_table):
    rows = 2 * SPAN
    outer_count, inner_count = lax.axis_size("outer"), lax.axis_size("inner")
    outer_index, inner_index = lax.axis_index("outer"), lax.axis_index("inner")

    def leading(a, b):
        source = (outer_index - a) % outer_count * inner_count + (inner_index - b) % inner_count
        return span_table[source, 0]

    steps = ((1, 0), (0, 1), (1, 1))
    own = leading(0, 0)
    halves = jnp.stack([(leading(a, b) > own).astype(jnp.int32) for a, b in steps])
    packed = jnp.concatenate([key_rows, value_rows], 0)
    arrived = [shifted(packed, a, b) for a, b in steps]
    log_two, row_dot = pl.pallas_call(
        prep_kernel,
        out_shape=(pltpu.VMEM((HEADS, rows), F32), pltpu.VMEM((HEADS, rows), F32)),
        in_specs=[VMEM] * 3,
        out_specs=(VMEM, VMEM),
        compiler_params=PARAMS,
        name="row_dots",
    )(out_grad, outputs, log_sum)
    returned, scores = [], []
    for j, (a, b) in enumerate(steps):
        part, first, second = pl.pallas_call(
            remote_kernel,
            out_shape=(
                jax.ShapeDtypeStruct((2 * rows, HD), BF16),
                pltpu.VMEM((SPAN, WIDE), BF16),
                pltpu.VMEM((SPAN, WIDE), BF16),
            ),
            in_specs=[SMEM] + [VMEM] * 5,
            out_specs=(VMEM, VMEM, VMEM),
            compiler_params=PARAMS,
            cost_estimate=units(2),
            name="remote_block",
        )(halves[j : j + 1], queries, out_grad, arrived[j], log_two, row_dot)
        returned.append(shifted(part, -a, -b))
        scores += [first, second]
    query_grad, key_own, value_own = pl.pallas_call(
        own_kernel,
        out_shape=(
            jax.ShapeDtypeStruct((rows, WIDE), BF16),
            pltpu.VMEM((rows, HD), F32),
            pltpu.VMEM((rows, HD), F32),
        ),
        in_specs=[SMEM] + [VMEM] * 14,
        out_specs=(VMEM, VMEM, VMEM),
        compiler_params=PARAMS,
        cost_estimate=units(4),
        name="own_block",
    )(halves, queries, out_grad, packed, log_two, row_dot, *arrived, *scores)
    key_total = key_own
    value_total = value_own
    for part in returned:
        key_total = key_total + part[:rows].astype(F32)
        value_total = value_total + part[rows:].astype(F32)
    return (query_grad, key_total * FACTOR, value_total)


def solution(mesh):
    tokens = P(("outer", "inner"), None)
    return jax.shard_map(
        per_device,
        mesh=mesh,
        in_specs=(tokens,) * 5 + (P(None, ("outer", "inner")), P()),
        out_specs=(tokens,) * 3,
        check_vma=False,
    )
```

time: 96.9 us -> 48.7 us (0.50)
  the two profiles are of different devices: /device:TPU:223 before, /device:TPU:1 now
where the time goes in v1:
time: 48.7 us; the launch traced here: 48.2 us
  starting transfers between devices  28.5 us (59%)
  Pallas kernels  8.83 us (18%)
  local copies, waits for them, and re-layouts  5.23 us (11%)
  between operations  4.76 us (10%)
  other arithmetic  0.84 us (2%)
    ppermute x6, starting transfers between devices, shifted(): return lax.ppermute(shard, ('outer', 'inner'), pairs)  28.5 us
    unnamed x13, local copies, waits for them, and re-layouts  4.55 us
    pallas_call x1, Pallas kernels, per_device(): pl.pallas_call(own_kernel, out_shape=(jax.ShapeDtypeStruct((rows, WIDE),...  4.31 us
    pallas_call x3, Pallas kernels, per_device(): pl.pallas_call(remote_kernel, out_shape=(jax.ShapeDtypeStruct((2 * rows,...  3.86 us
  transfers between devices with their start and end apart: 6, of which 0 were waited for; matrix products, arithmetic and copies ran while one was open for 2% of the time, Pallas kernels for 18%

profile of v1, /device:TPU:1, one launch (start us, length us, event | category | flops | bytes accessed | tf_op | source)
XLA Modules:
  0.0 48.2 jit_solution(6567434353606550902)
XLA Ops:
  0.6 0.0 copy-start.4
  0.6 0.9 %constant_dynamic-update-slice_fusion.1 = bf16[512,128]{1,0:T(8,128)(2,1)S(1)} fusion(bf16[256,128]{1,0:T(8,128)(2,1)} %param.8), kind=kLoop, calls=%fused_computation.3 | loop fusion | bytes 131072
  1.5 0.0 copy-done.4
  1.5 3.9 %collective-permute-start = (bf16[512,128]{1,0:T(8,128)(2,1)S(1)}, bf16[512,128]{1,0:T(8,128)(2,1)S(1)}, u32[]{:S(2)}, u32[]{:S(2)}) collective-permute-start(bf16[512,128]{1,0:T(8,128)(2,1)S(1)} %constant_dynamic-update-slice_fusion.kv_ref), channel_id=1, source_target_pairs={{0,32},{1,33},{2,34},{3,35},{4,36},{5,37},{6,38},{7,39},{8,40},{9,... | collective-permute-start | bytes 393224 | tf_op jit(solution)/shard_map/ppermute | solution.py:155
  5.5 5.2 %collective-permute-start.1 = (bf16[512,128]{1,0:T(8,128)(2,1)S(1)}, bf16[512,128]{1,0:T(8,128)(2,1)S(1)}, u32[]{:S(2)}, u32[]{:S(2)}) collective-permute-start(bf16[512,128]{1,0:T(8,128)(2,1)S(1)} %constant_dynamic-update-slice_fusion.kv_ref), channel_id=1, source_target_pairs={{0,1},{1,2},{2,3},{3,4},{4,5},{5,6},{6,7},{7,8},{8,9},{9,10},{10,1... | collective-permute-start | bytes 393224 | tf_op jit(solution)/shard_map/ppermute | solution.py:155
  10.7 2.3 %collective-permute-start.2 = (bf16[512,128]{1,0:T(8,128)(2,1)S(1)}, bf16[512,128]{1,0:T(8,128)(2,1)S(1)}, u32[]{:S(2)}, u32[]{:S(2)}) collective-permute-start(bf16[512,128]{1,0:T(8,128)(2,1)S(1)} %constant_dynamic-update-slice_fusion.kv_ref), channel_id=1, source_target_pairs={{0,33},{1,34},{2,35},{3,36},{4,37},{5,38},{6,39},{7,40},{8,41},{9,... | collective-permute-start | bytes 393224 | tf_op jit(solution)/shard_map/ppermute | solution.py:155
  13.1 0.0 copy-start.5
  13.1 0.0 copy-start.3
  13.1 0.7 %copy-done.5 = s32[512,2]{0,1:T(2,128)S(1)} copy-done((s32[512,2]{0,1:T(2,128)S(1)}, s32[512,2]{0,1:T(2,128)}, u32[]{:S(2)}) %copy-start.5) | copy-done | bytes 4120
  13.8 0.7 %constant_dynamic-slice_fusion.3 = (s32[1,1]{0,1:T(1,128)}, s32[1,1]{0,1:T(1,128)}, s32[1,1]{0,1:T(1,128)}, s32[1,1]{0,1:T(1,128)}) fusion(s32[512,2]{0,1:T(2,128)S(1)} %copy-done.5, s32[]{:T(128)S(6)} %select_n.41, s32[]{:T(128)S(6)} %select_n.43, s32[]{:T(128)S(6)} %select_n.46, s32[]{:T(128)S(6)} %select_n.45), kind=kLoop, calls=%fused_computation.7 | loop fusion | bytes 48 | tf_op jit(solution)/shard_map/dynamic_slice | solution.py:165
  18.3 0.0 copy-done.3
  18.4 0.0 copy-start
  18.4 1.2 %copy-done = bf16[256,2048]{1,0:T(8,128)(2,1)S(1)} copy-done((bf16[256,2048]{1,0:T(8,128)(2,1)S(1)}, bf16[256,2048]{1,0:T(8,128)(2,1)}, u32[]{:S(2)}) %copy-start) | copy-done | bytes 1048600
  19.6 0.0 copy-start.1
  19.6 1.2 %copy-done.1 = bf16[256,2048]{1,0:T(8,128)(2,1)S(1)} copy-done((bf16[256,2048]{1,0:T(8,128)(2,1)S(1)}, bf16[256,2048]{1,0:T(8,128)(2,1)}, u32[]{:S(2)}) %copy-start.1) | copy-done | bytes 1048600
  20.8 0.0 copy-start.2
  20.8 0.7 %row_dots.1 = (f32[16,256]{1,0:T(8,128)S(1)}, f32[16,256]{1,0:T(8,128)S(1)}) custom-call(bf16[256,2048]{1,0:T(8,128)(2,1)S(1)} %copy-done, bf16[256,2048]{1,0:T(8,128)(2,1)S(1)} %copy-done.1, f32[16,256]{1,0:T(8,128)S(1)} %copy-done.3), custom_call_target="tpu_custom_call" | custom-call | tf_op jit(solution)/shard_map/row_dots/pallas_call | solution.py:172
  21.5 0.0 collective-permute-done.kv_ref.kv1_ref
  21.5 0.6 %copy-done.2 = bf16[256,2048]{1,0:T(8,128)(2,1)S(1)} copy-done((bf16[256,2048]{1,0:T(8,128)(2,1)S(1)}, bf16[256,2048]{1,0:T(8,128)(2,1)}, u32[]{:S(2)}) %copy-start.2) | copy-done | bytes 1048600
  22.0 1.3 %remote_block.3 = (bf16[512,128]{1,0:T(8,128)(2,1)S(1)}, bf16[128,2048]{1,0:T(8,128)(2,1)S(1)}, bf16[128,2048]{1,0:T(8,128)(2,1)S(1)}) custom-call(s32[1]{0:T(128)} %bitcast.half_ref, bf16[256,2048]{1,0:T(8,128)(2,1)S(1)} %copy-done.2, bf16[256,2048]{1,0:T(8,128)(2,1)S(1)} %copy-done, bf16[512,128]{1,0:T(8,128)(2,1)S(1)} %collective-permute-done.kv_ref.kv1_ref, ...), custom_call_target="tpu_custom_call" | custom-call | flops 671088640 | bytes 1048576 | tf_op jit(solution)/shard_map/remote_block/pallas_call | solution.py:182
  23.3 3.6 %collective-permute-start.3 = (bf16[512,128]{1,0:T(8,128)(2,1)S(1)}, bf16[512,128]{1,0:T(8,128)(2,1)S(1)}, u32[]{:S(2)}, u32[]{:S(2)}) collective-permute-start(bf16[512,128]{1,0:T(8,128)(2,1)S(1)} %get-tuple-element.27), channel_id=1, source_target_pairs={{0,480},{1,481},{2,482},{3,483},{4,484},{5,485},{6,486},{7,487},{8... | collective-permute-start | bytes 393224 | tf_op jit(solution)/shard_map/ppermute | solution.py:155
  26.9 0.0 collective-permute-done.1.kv_ref.kv2_ref
  26.9 1.3 %remote_block.4 = (bf16[512,128]{1,0:T(8,128)(2,1)S(1)}, bf16[128,2048]{1,0:T(8,128)(2,1)S(1)}, bf16[128,2048]{1,0:T(8,128)(2,1)S(1)}) custom-call(s32[1]{0:T(128)} %bitcast.1.half_ref, bf16[256,2048]{1,0:T(8,128)(2,1)S(1)} %copy-done.2, bf16[256,2048]{1,0:T(8,128)(2,1)S(1)} %copy-done, bf16[512,128]{1,0:T(8,128)(2,1)S(1)} %collective-permute-done.1.kv_ref.kv2_ref, ...), custom_call_target="tpu_custom_call" | custom-call | flops 671088640 | bytes 1048576 | tf_op jit(solution)/shard_map/remote_block/pallas_call | solution.py:182
  28.2 5.5 %collective-permute-start.4 = (bf16[512,128]{1,0:T(8,128)(2,1)S(1)}, bf16[512,128]{1,0:T(8,128)(2,1)S(1)}, u32[]{:S(2)}, u32[]{:S(2)}) collective-permute-start(bf16[512,128]{1,0:T(8,128)(2,1)S(1)} %get-tuple-element.28), channel_id=1, source_target_pairs={{0,31},{1,0},{2,1},{3,2},{4,3},{5,4},{6,5},{7,6},{8,7},{9,8},{10,9... | collective-permute-start | bytes 393224 | tf_op jit(solution)/shard_map/ppermute | solution.py:155
  33.8 0.0 collective-permute-done.2.kv_ref.kv3_ref
  33.8 1.3 %remote_block.5 = (bf16[512,128]{1,0:T(8,128)(2,1)S(1)}, bf16[128,2048]{1,0:T(8,128)(2,1)S(1)}, bf16[128,2048]{1,0:T(8,128)(2,1)S(1)}) custom-call(s32[1]{0:T(128)} %bitcast.2.half_ref, bf16[256,2048]{1,0:T(8,128)(2,1)S(1)} %copy-done.2, bf16[256,2048]{1,0:T(8,128)(2,1)S(1)} %copy-done, bf16[512,128]{1,0:T(8,128)(2,1)S(1)} %collective-permute-done.2.kv_ref.kv3_ref, ...), custom_call_target="tpu_custom_call" | custom-call | flops 671088640 | bytes 1048576 | tf_op jit(solution)/shard_map/remote_block/pallas_call | solution.py:182
  35.1 7.9 %collective-permute-start.5 = (bf16[512,128]{1,0:T(8,128)(2,1)S(1)}, bf16[512,128]{1,0:T(8,128)(2,1)S(1)}, u32[]{:S(2)}, u32[]{:S(2)}) collective-permute-start(bf16[512,128]{1,0:T(8,128)(2,1)S(1)} %get-tuple-element.29), channel_id=1, source_target_pairs={{0,511},{1,480},{2,481},{3,482},{4,483},{5,484},{6,485},{7,486},{8... | collective-permute-start | bytes 393224 | tf_op jit(solution)/shard_map/ppermute | solution.py:155
  43.0 0.1 pad_add_fusion.half_ref
  43.1 4.3 %own_block.1 = (bf16[256,2048]{1,0:T(8,128)(2,1)}, f32[256,128]{1,0:T(8,128)S(1)}, f32[256,128]{1,0:T(8,128)S(1)}) custom-call(s32[3]{0:T(128)S(1)} %pad_add_fusion.half_ref, bf16[256,2048]{1,0:T(8,128)(2,1)S(1)} %copy-done.2, bf16[256,2048]{1,0:T(8,128)(2,1)S(1)} %copy-done, bf16[512,128]{1,0:T(8,128)(2,1)S(1)} %constant_dynamic-update-slice_fusion.kv_ref, ...), custom_call_target="tpu_custom_call" | custom-call | flops 1342177280 | bytes 1048576 | tf_op jit(solution)/shard_map/own_block/pallas_call | solution.py:197
  47.4 0.0 collective-permute-done.3
  47.4 0.0 collective-permute-done.4
  47.4 0.0 collective-permute-done.5
  47.4 0.8 %convert_add_fusion = (f32[256,128]{1,0:T(8,128)}, f32[256,128]{1,0:T(8,128)}) fusion(f32[256,128]{1,0:T(8,128)S(1)} %get-tuple-element.30, bf16[512,128]{1,0:T(8,128)(2,1)S(1)} %collective-permute-done.5, bf16[512,128]{1,0:T(8,128)(2,1)S(1)} %collective-permute-done.4, bf16[512,128]{1,0:T(8,128)(2,1)S(1)} %collective-permute-done.3, ...), kind=kLoop, calls=%fused_computation | loop fusion | flops 425984 | bytes 917504 | tf_op jit(solution)/shard_map/add | solution.py:214
  (1 shorter events, 0.0 us)
Async XLA Ops:
  0.6 0.9 %copy-start.4 = (bf16[256,128]{1,0:T(8,128)(2,1)S(1)}, bf16[256,128]{1,0:T(8,128)(2,1)}, u32[]{:S(2)}) copy-start(bf16[256,128]{1,0:T(8,128)(2,1)} %param.9) | copy-start | bytes 196612
  1.5 20.0 %collective-permute-start = (bf16[512,128]{1,0:T(8,128)(2,1)S(1)}, bf16[512,128]{1,0:T(8,128)(2,1)S(1)}, u32[]{:S(2)}, u32[]{:S(2)}) collective-permute-start(bf16[512,128]{1,0:T(8,128)(2,1)S(1)} %constant_dynamic-update-slice_fusion.kv_ref), channel_id=1, source_target_pairs={{0,32},{1,33},{2,34},{3,35},{4,36},{5,37},{6,38},{7,39},{8,40},{9,... | collective-permute-start | bytes 393224 | tf_op jit(solution)/shard_map/ppermute | solution.py:155
  5.5 21.4 %collective-permute-start.1 = (bf16[512,128]{1,0:T(8,128)(2,1)S(1)}, bf16[512,128]{1,0:T(8,128)(2,1)S(1)}, u32[]{:S(2)}, u32[]{:S(2)}) collective-permute-start(bf16[512,128]{1,0:T(8,128)(2,1)S(1)} %constant_dynamic-update-slice_fusion.kv_ref), channel_id=1, source_target_pairs={{0,1},{1,2},{2,3},{3,4},{4,5},{5,6},{6,7},{7,8},{8,9},{9,10},{10,1... | collective-permute-start | bytes 393224 | tf_op jit(solution)/shard_map/ppermute | solution.py:155
  10.7 23.1 %collective-permute-start.2 = (bf16[512,128]{1,0:T(8,128)(2,1)S(1)}, bf16[512,128]{1,0:T(8,128)(2,1)S(1)}, u32[]{:S(2)}, u32[]{:S(2)}) collective-permute-start(bf16[512,128]{1,0:T(8,128)(2,1)S(1)} %constant_dynamic-update-slice_fusion.kv_ref), channel_id=1, source_target_pairs={{0,33},{1,34},{2,35},{3,36},{4,37},{5,38},{6,39},{7,40},{8,41},{9,... | collective-permute-start | bytes 393224 | tf_op jit(solution)/shard_map/ppermute | solution.py:155
  13.1 0.7 %copy-start.5 = (s32[512,2]{0,1:T(2,128)S(1)}, s32[512,2]{0,1:T(2,128)}, u32[]{:S(2)}) copy-start(s32[512,2]{0,1:T(2,128)} %param.13) | copy-start | bytes 12292
  13.1 5.3 %copy-start.3 = (f32[16,256]{1,0:T(8,128)S(1)}, f32[16,256]{1,0:T(8,128)}, u32[]{:S(2)}) copy-start(f32[16,256]{1,0:T(8,128)} %log_ref.1) | copy-start | bytes 49156
  18.4 1.2 %copy-start = (bf16[256,2048]{1,0:T(8,128)(2,1)S(1)}, bf16[256,2048]{1,0:T(8,128)(2,1)}, u32[]{:S(2)}) copy-start(bf16[256,2048]{1,0:T(8,128)(2,1)} %grad_ref.9) | copy-start | bytes 3145732
  19.6 1.2 %copy-start.1 = (bf16[256,2048]{1,0:T(8,128)(2,1)S(1)}, bf16[256,2048]{1,0:T(8,128)(2,1)}, u32[]{:S(2)}) copy-start(bf16[256,2048]{1,0:T(8,128)(2,1)} %out_ref.1) | copy-start | bytes 3145732
  20.8 1.2 %copy-start.2 = (bf16[256,2048]{1,0:T(8,128)(2,1)S(1)}, bf16[256,2048]{1,0:T(8,128)(2,1)}, u32[]{:S(2)}) copy-start(bf16[256,2048]{1,0:T(8,128)(2,1)} %query_ref.7) | copy-start | bytes 3145732
  23.3 24.1 %collective-permute-start.3 = (bf16[512,128]{1,0:T(8,128)(2,1)S(1)}, bf16[512,128]{1,0:T(8,128)(2,1)S(1)}, u32[]{:S(2)}, u32[]{:S(2)}) collective-permute-start(bf16[512,128]{1,0:T(8,128)(2,1)S(1)} %get-tuple-element.27), channel_id=1, source_target_pairs={{0,480},{1,481},{2,482},{3,483},{4,484},{5,485},{6,486},{7,487},{8... | collective-permute-start | bytes 393224 | tf_op jit(solution)/shard_map/ppermute | solution.py:155
  28.2 19.2 %collective-permute-start.4 = (bf16[512,128]{1,0:T(8,128)(2,1)S(1)}, bf16[512,128]{1,0:T(8,128)(2,1)S(1)}, u32[]{:S(2)}, u32[]{:S(2)}) collective-permute-start(bf16[512,128]{1,0:T(8,128)(2,1)S(1)} %get-tuple-element.28), channel_id=1, source_target_pairs={{0,31},{1,0},{2,1},{3,2},{4,3},{5,4},{6,5},{7,6},{8,7},{9,8},{10,9... | collective-permute-start | bytes 393224 | tf_op jit(solution)/shard_map/ppermute | solution.py:155
  35.1 12.3 %collective-permute-start.5 = (bf16[512,128]{1,0:T(8,128)(2,1)S(1)}, bf16[512,128]{1,0:T(8,128)(2,1)S(1)}, u32[]{:S(2)}, u32[]{:S(2)}) collective-permute-start(bf16[512,128]{1,0:T(8,128)(2,1)S(1)} %get-tuple-element.29), channel_id=1, source_target_pairs={{0,511},{1,480},{2,481},{3,482},{4,483},{5,484},{6,485},{7,486},{8... | collective-permute-start | bytes 393224 | tf_op jit(solution)/shard_map/ppermute | solution.py:155

commit v2 on v1

v2 whole, which is shorter than its diff:
```python
import functools
import math

import jax
import jax.numpy as jnp
from jax import lax
from jax.experimental import pallas as pl
from jax.experimental.pallas import tpu as pltpu
from jax.sharding import PartitionSpec as P

F32 = jnp.float32
BF16 = jnp.bfloat16
HEADS = 16
HD = 128
SPAN = 128
WIDE = HEADS * HD
FACTOR = 1.0 / math.sqrt(HD)
OUTER = 16
INNER = 32
STEPS = ((1, 0), (0, 1), (1, 1))
LOG2E = math.log2(math.e)


def dot(a, b, contract):
    return lax.dot_general(a, b, ((contract[:1], contract[1:]), ((), ())), preferred_element_type=F32)


def stacked(ref, rows):
    return jnp.concatenate([ref[rows, h * HD : (h + 1) * HD] for h in range(HEADS)], 0)


def sub_block(key, value, query_ref, grad_ref, rows, log_two, row_dot, mask=None, ready=None):
    probs, dscores = [], []
    for m in range(0, HEADS, 2):
        if ready is not None:
            ready(m)
        one, two = slice(m * HD, (m + 1) * HD), slice((m + 1) * HD, (m + 2) * HD)
        pair = jnp.concatenate([query_ref[rows, one], query_ref[rows, two]], 0)
        grad = jnp.concatenate([grad_ref[rows, one], grad_ref[rows, two]], 0)
        lanes = lambda of: jnp.concatenate([of(m), of(m + 1)], 1)
        scores = dot(key, pair, (1, 1))
        weights = jnp.exp2(scores * (FACTOR * LOG2E) - lanes(log_two))
        if mask is not None:
            weights = jnp.where(mask, weights, 0.0)
        dweights = dot(value, grad, (1, 1))
        probs.append(weights.astype(BF16))
        dscores.append((weights * (dweights - lanes(row_dot))).astype(BF16))
    return jnp.concatenate(probs, 1), jnp.concatenate(dscores, 1)


def of_rows(ref, rows):
    return lambda h: ref[h : h + 1, rows]


def of_half(ref, is_low):
    return lambda h: jnp.where(is_low, ref[h : h + 1, 0:SPAN], ref[h : h + 1, SPAN:])


def pack_kernel(
    place_ref,
    table_hbm,
    key_hbm,
    value_hbm,
    query_hbm,
    grad_hbm,
    out_hbm,
    sum_hbm,
    packed_ref,
    halves_ref,
    log_ref,
    dot_ref,
    query_ref,
    grad_ref,
    out_ref,
    sum_ref,
    table_ref,
    sems,
):
    rows = 2 * SPAN
    copies = [
        pltpu.make_async_copy(table_hbm, table_ref, sems.at[2]),
        pltpu.make_async_copy(key_hbm, packed_ref.at[0:rows], sems.at[0]),
        pltpu.make_async_copy(value_hbm, packed_ref.at[rows : 2 * rows], sems.at[1]),
    ]
    for copy in copies:
        copy.start()
    pairs = ((sum_hbm, sum_ref), (grad_hbm, grad_ref), (out_hbm, out_ref), (query_hbm, query_ref))
    wide = [pltpu.make_async_copy(source, target, sems.at[i + 3]) for i, (source, target) in enumerate(pairs)]
    for copy in wide:
        copy.start()
    outer, inner = place_ref[0] // INNER, place_ref[0] % INNER
    copies[0].wait()
    own = table_ref[0, outer * INNER + inner]
    for j, (a, b) in enumerate(STEPS):
        source = (outer - a + OUTER) % OUTER * INNER + (inner - b + INNER) % INNER
        halves_ref[j] = (table_ref[0, source] > own).astype(jnp.int32)
    copies[1].wait()
    copies[2].wait()
    wide[0].wait()
    log_ref[...] = sum_ref[...] * LOG2E
    wide[1].wait()
    wide[2].wait()
    dot_ref[...] = row_dots(grad_ref, out_ref)
    wide[3].wait()


def row_dots(grad_ref, out_ref):
    columns = []
    for h in range(HEADS):
        one = slice(h * HD, (h + 1) * HD)
        product = grad_ref[:, one].astype(F32) * out_ref[:, one].astype(F32)
        columns.append(jnp.sum(product, axis=1, keepdims=True))
    return jnp.concatenate(columns, 1).T


def remote_kernel(j, half_ref, query_ref, grad_ref, kv_ref, log_ref, dot_ref, part_ref, first_ref, second_ref):
    remote_block(j, half_ref, query_ref, grad_ref, kv_ref, log_ref, dot_ref, part_ref, first_ref, second_ref)


def remote_block(j, half_ref, query_ref, grad_ref, kv_ref, log_ref, dot_ref, part_ref, first_ref, second_ref, ready=None):
    half = half_ref[j]
    rows = pl.ds(pl.multiple_of(half * SPAN, SPAN), SPAN)
    high = slice(SPAN, 2 * SPAN)
    key, value = kv_ref[0:SPAN, :], kv_ref[2 * SPAN : 3 * SPAN, :]
    probs, dscores = sub_block(
        key, value, query_ref, grad_ref, high, of_rows(log_ref, high), of_rows(dot_ref, high), ready=ready
    )
    first_ref[...] = dscores
    key_low = dot(dscores, stacked(query_ref, high), (1, 0))
    value_low = dot(probs, stacked(grad_ref, high), (1, 0))
    is_low = half == 0
    key, value = kv_ref[rows, :], kv_ref[pl.ds(pl.multiple_of((half + 2) * SPAN, SPAN), SPAN), :]
    probs, dscores = sub_block(
        key, value, query_ref, grad_ref, rows, of_half(log_ref, is_low), of_half(dot_ref, is_low)
    )
    second_ref[...] = dscores
    key_half = dot(dscores, stacked(query_ref, rows), (1, 0))
    value_half = dot(probs, stacked(grad_ref, rows), (1, 0))
    part_ref[0:SPAN, :] = (key_low + jnp.where(is_low, key_half, 0.0)).astype(BF16)
    part_ref[SPAN : 2 * SPAN, :] = jnp.where(is_low, 0.0, key_half).astype(BF16)
    part_ref[2 * SPAN : 3 * SPAN, :] = (value_low + jnp.where(is_low, value_half, 0.0)).astype(BF16)
    part_ref[3 * SPAN :, :] = jnp.where(is_low, 0.0, value_half).astype(BF16)


def own_kernel(
    half_ref,
    query_ref,
    grad_ref,
    kv_ref,
    log_ref,
    dot_ref,
    kv1_ref,
    kv2_ref,
    kv3_ref,
    first1_ref,
    second1_ref,
    first2_ref,
    second2_ref,
    first3_ref,
    second3_ref,
    query_grad_hbm,
    key_grad_ref,
    value_grad_ref,
    query_grad_ref,
    sems,
):
    low, high = slice(0, SPAN), slice(SPAN, 2 * SPAN)
    span = (SPAN, 2 * SPAN)
    keys = lax.broadcasted_iota(jnp.int32, span, 0)
    mask = keys <= lax.rem(lax.broadcasted_iota(jnp.int32, span, 1), SPAN)
    key_low, key_high = kv_ref[low, :], kv_ref[high, :]
    value_low, value_high = kv_ref[2 * SPAN : 3 * SPAN, :], kv_ref[3 * SPAN :, :]

    def block(key, value, rows, mask=None):
        probs, dscores = sub_block(
            key, value, query_ref, grad_ref, rows, of_rows(log_ref, rows), of_rows(dot_ref, rows), mask
        )
        key_part = dot(dscores, stacked(query_ref, rows), (1, 0))
        return key_part, dot(probs, stacked(grad_ref, rows), (1, 0)), dscores

    zero = jnp.zeros((SPAN, HD), BF16)
    remotes = ((kv1_ref, first1_ref, second1_ref), (kv2_ref, first2_ref, second2_ref), (kv3_ref, first3_ref, second3_ref))

    def query_part(rows, keys, scores):
        total = dot(jnp.concatenate(keys, 0).T, jnp.concatenate(scores, 0), (1, 0)) * FACTOR
        for h in range(HEADS):
            one = slice(h * HD, (h + 1) * HD)
            query_grad_ref[rows, one] = total[:, one].T.astype(BF16)
        copy = pltpu.make_async_copy(query_grad_ref.at[rows], query_grad_hbm.at[rows], sems.at[rows.start // SPAN])
        copy.start()
        return copy

    key_lh, value_lh, ds_lh = block(key_low, value_low, high)
    key_hh, value_hh, ds_hh = block(key_high, value_high, high, mask)
    keys, scores = [key_low, key_high], [ds_lh, ds_hh]
    for j, (ref, first, second) in enumerate(remotes):
        keys += [ref[low, :], jnp.where(half_ref[j] == 0, zero, ref[high, :])]
        scores += [first[...], second[...]]
    copy_high = query_part(high, keys, scores)
    key_ll, value_ll, ds_ll = block(key_low, value_low, low, mask)
    keys, scores = [key_low], [ds_ll]
    for j, (ref, first, second) in enumerate(remotes):
        keys.append(jnp.where(half_ref[j] == 0, ref[low, :], zero))
        scores.append(second[...])
    copy_low = query_part(low, keys, scores)
    key_grad_ref[low, :] = key_ll + key_lh
    key_grad_ref[high, :] = key_hh
    value_grad_ref[low, :] = value_ll + value_lh
    value_grad_ref[high, :] = value_hh
    copy_high.wait()
    copy_low.wait()


VMEM = pl.BlockSpec(memory_space=pltpu.VMEM)
ANY = pl.BlockSpec(memory_space=pl.ANY)
SMEM = pl.BlockSpec(memory_space=pltpu.SMEM)
PARAMS = pltpu.CompilerParams(vmem_limit_bytes=24 << 20)


def units(count):
    return pl.CostEstimate(flops=count * 10 * SPAN * HD * SPAN * HEADS, bytes_accessed=1 << 20, transcendentals=count * SPAN * SPAN * HEADS)


def shifted(shard, by_outer, by_inner):
    outer, inner = lax.axis_size("outer"), lax.axis_size("inner")
    pairs = [
        (o * inner + i, (o + by_outer) % outer * inner + (i + by_inner) % inner) for o in range(outer) for i in range(inner)
    ]
    return lax.ppermute(shard, ("outer", "inner"), pairs)


def per_device(queries, key_rows, value_rows, out_grad, outputs, log_sum, span_table):
    rows = 2 * SPAN
    place = lax.axis_index(("outer", "inner")).reshape(1)
    table, key_rows, value_rows, queries, out_grad, outputs, log_sum = (
        pltpu.with_memory_space_constraint(x, pltpu.HBM)
        for x in (span_table.T, key_rows, value_rows, queries, out_grad, outputs, log_sum)
    )
    packed, halves, log_two, row_dot, queries, out_grad = pl.pallas_call(
        pack_kernel,
        out_shape=(
            pltpu.VMEM((2 * rows, HD), BF16),
            pltpu.SMEM((len(STEPS),), jnp.int32),
            pltpu.VMEM((HEADS, rows), F32),
            pltpu.VMEM((HEADS, rows), F32),
            pltpu.VMEM((rows, WIDE), BF16),
            pltpu.VMEM((rows, WIDE), BF16),
        ),
        in_specs=[SMEM] + [ANY] * 7,
        out_specs=(VMEM, SMEM) + (VMEM,) * 4,
        scratch_shapes=[
            pltpu.VMEM((rows, WIDE), BF16),
            pltpu.VMEM((HEADS, rows), F32),
            pltpu.SMEM((2, OUTER * INNER), jnp.int32),
            pltpu.SemaphoreType.DMA((7,)),
        ],
        compiler_params=PARAMS,
        name="pack",
    )(place, table, key_rows, value_rows, queries, out_grad, outputs, log_sum)
    arrived = [shifted(packed, a, b) for a, b in STEPS]
    returned, scores = [], []
    for j, (a, b) in enumerate(STEPS):
        part, first, second = pl.pallas_call(
            functools.partial(remote_kernel, j),
            out_shape=(
                pltpu.VMEM((2 * rows, HD), BF16),
                pltpu.VMEM((SPAN, WIDE), BF16),
                pltpu.VMEM((SPAN, WIDE), BF16),
            ),
            in_specs=[SMEM] + [VMEM] * 5,
            out_specs=(VMEM,) * 3,
            compiler_params=PARAMS,
            cost_estimate=units(2),
            name="remote_block",
        )(halves, queries, out_grad, arrived[j], log_two, row_dot)
        returned.append(shifted(part, -a, -b))
        scores += [first, second]
    query_grad, key_own, value_own = pl.pallas_call(
        own_kernel,
        out_shape=(
            pltpu.HBM((rows, WIDE), BF16),
            pltpu.VMEM((rows, HD), F32),
            pltpu.VMEM((rows, HD), F32),
        ),
        in_specs=[SMEM] + [VMEM] * 14,
        out_specs=(ANY, VMEM, VMEM),
        scratch_shapes=[pltpu.VMEM((rows, WIDE), BF16), pltpu.SemaphoreType.DMA((2,))],
        compiler_params=PARAMS,
        cost_estimate=units(4),
        name="own_block",
    )(halves, queries, out_grad, packed, log_two, row_dot, *arrived, *scores)
    key_total = key_own
    value_total = value_own
    for part in returned:
        key_total = key_total + part[:rows].astype(F32)
        value_total = value_total + part[rows:].astype(F32)
    return (query_grad, key_total * FACTOR, value_total)


def solution(mesh):
    tokens = P(("outer", "inner"), None)
    return jax.shard_map(
        per_device,
        mesh=mesh,
        in_specs=(tokens,) * 5 + (P(None, ("outer", "inner")), P()),
        out_specs=(tokens,) * 3,
        check_vma=False,
    )
```

time: 48.7 us -> 40.6 us (0.83)
  local copies, waits for them, and re-layouts: 5.23 us -> 0 us
  between operations: 4.76 us -> 0.76 us
  Pallas kernels: 8.83 us -> 9.87 us
    unnamed x13 -> x0, local copies, waits for them, and re-layouts: 4.55 us -> none
    pallas_call x5, Pallas kernels: 8.83 us -> 9.87 us  [the longest x3 3.97 us: per_device(): pl.pallas_call(functools.partial(remote_kernel, j), out_shape=(pltpu.VMEM...]
    dynamic_slice x1 -> x0, local copies, waits for them, and re-layouts: 0.67 us -> none  [leading(): return span_table[source, 0]]
  transfers between devices with their start and end apart: 6 -> 6, of which waited for: 0 -> 0; matrix products, arithmetic and copies ran while one was open for 2% -> 0% of each run, Pallas kernels for 18% -> 19%
where the time goes in v2:
time: 40.6 us; the launch traced here: 40.3 us
  starting transfers between devices  28.9 us (71%)
  Pallas kernels  9.87 us (24%)
  other arithmetic  0.76 us (2%)
  between operations  0.76 us (2%)
    ppermute x6, starting transfers between devices, shifted(): return lax.ppermute(shard, ('outer', 'inner'), pairs)  28.9 us
    pallas_call x3, Pallas kernels, per_device(): pl.pallas_call(functools.partial(remote_kernel, j), out_shape=(pltpu.VMEM...  3.97 us
    pallas_call x1, Pallas kernels, per_device(): pl.pallas_call(own_kernel, out_shape=(pltpu.HBM((rows, WIDE), BF16), pltp...  3.53 us
    pallas_call x1, Pallas kernels, per_device(): pl.pallas_call(pack_kernel, out_shape=(pltpu.VMEM((2 * rows, HD), BF16),...  2.37 us
  transfers between devices with their start and end apart: 6, of which 0 were waited for; matrix products, arithmetic and copies ran while one was open for 0% of the time, Pallas kernels for 19%

profile of v2, /device:TPU:1, one launch (start us, length us, event | category | flops | bytes accessed | tf_op | source)
XLA Modules:
  0.0 40.3 jit_solution(14980113844193224536)
XLA Ops:
  0.6 2.4 %pack.1 = (bf16[512,128]{1,0:T(8,128)(2,1)S(1)}, s32[3]{0:T(128)S(4)}, f32[16,256]{1,0:T(8,128)S(1)}, f32[16,256]{1,0:T(8,128)S(1)}, bf16[256,2048]{1,0:T(8,128)(2,1)S(1)}, /*index=5*/bf16[256,2048]{1,0:T(8,128)(2,1)S(1)}) custom-call(s32[1]{0:T(128)} %bitcast.place_ref, s32[2,512]{1,0:T(2,128)} %bitcast.2, bf16[256,128]{1,0:T(8,128)(2,1)} %key_hbm.1, ...), custom_call_target="tpu_custom_call" | custom-call | tf_op jit(solution)/shard_map/pack/pallas_call | solution.py:239
  3.0 3.9 %collective-permute-start = (bf16[512,128]{1,0:T(8,128)(2,1)S(1)}, bf16[512,128]{1,0:T(8,128)(2,1)S(1)}, u32[]{:S(2)}, u32[]{:S(2)}) collective-permute-start(bf16[512,128]{1,0:T(8,128)(2,1)S(1)} %get-tuple-element.24.kv_ref), channel_id=1, source_target_pairs={{0,32},{1,33},{2,34},{3,35},{4,36},{5,37},{6,38},{7,39},{8,40},{9,... | collective-permute-start | bytes 393224 | tf_op jit(solution)/shard_map/ppermute | solution.py:229
  7.0 5.2 %collective-permute-start.1 = (bf16[512,128]{1,0:T(8,128)(2,1)S(1)}, bf16[512,128]{1,0:T(8,128)(2,1)S(1)}, u32[]{:S(2)}, u32[]{:S(2)}) collective-permute-start(bf16[512,128]{1,0:T(8,128)(2,1)S(1)} %get-tuple-element.24.kv_ref), channel_id=1, source_target_pairs={{0,1},{1,2},{2,3},{3,4},{4,5},{5,6},{6,7},{7,8},{8,9},{9,10},{10,1... | collective-permute-start | bytes 393224 | tf_op jit(solution)/shard_map/ppermute | solution.py:229
  12.2 2.3 %collective-permute-start.2 = (bf16[512,128]{1,0:T(8,128)(2,1)S(1)}, bf16[512,128]{1,0:T(8,128)(2,1)S(1)}, u32[]{:S(2)}, u32[]{:S(2)}) collective-permute-start(bf16[512,128]{1,0:T(8,128)(2,1)S(1)} %get-tuple-element.24.kv_ref), channel_id=1, source_target_pairs={{0,33},{1,34},{2,35},{3,36},{4,37},{5,38},{6,39},{7,40},{8,41},{9,... | collective-permute-start | bytes 393224 | tf_op jit(solution)/shard_map/ppermute | solution.py:229
  14.5 0.0 collective-permute-done.kv_ref.kv1_ref
  14.5 1.3 %remote_block.3 = (bf16[512,128]{1,0:T(8,128)(2,1)S(1)}, bf16[128,2048]{1,0:T(8,128)(2,1)S(1)}, bf16[128,2048]{1,0:T(8,128)(2,1)S(1)}) custom-call(s32[3]{0:T(128)S(4)} %get-tuple-element.21.half_ref, bf16[256,2048]{1,0:T(8,128)(2,1)S(1)} %get-tuple-element.22.query_ref, bf16[256,2048]{1,0:T(8,128)(2,1)S(1)} %get-tuple-element.23.grad_ref, ...), custom_call_target="tpu_custom_call" | custom-call | flops 671088640 | bytes 1048576 | tf_op jit(solution)/shard_map/remote_block/pallas_call | solution.py:263
  15.8 3.6 %collective-permute-start.3 = (bf16[512,128]{1,0:T(8,128)(2,1)S(1)}, bf16[512,128]{1,0:T(8,128)(2,1)S(1)}, u32[]{:S(2)}, u32[]{:S(2)}) collective-permute-start(bf16[512,128]{1,0:T(8,128)(2,1)S(1)} %get-tuple-element.35), channel_id=1, source_target_pairs={{0,480},{1,481},{2,482},{3,483},{4,484},{5,485},{6,486},{7,487},{8... | collective-permute-start | bytes 393224 | tf_op jit(solution)/shard_map/ppermute | solution.py:229
  19.4 0.0 collective-permute-done.1.kv_ref.kv2_ref
  19.4 1.3 %remote_block.4 = (bf16[512,128]{1,0:T(8,128)(2,1)S(1)}, bf16[128,2048]{1,0:T(8,128)(2,1)S(1)}, bf16[128,2048]{1,0:T(8,128)(2,1)S(1)}) custom-call(s32[3]{0:T(128)S(4)} %get-tuple-element.21.half_ref, bf16[256,2048]{1,0:T(8,128)(2,1)S(1)} %get-tuple-element.22.query_ref, bf16[256,2048]{1,0:T(8,128)(2,1)S(1)} %get-tuple-element.23.grad_ref, ...), custom_call_target="tpu_custom_call" | custom-call | flops 671088640 | bytes 1048576 | tf_op jit(solution)/shard_map/remote_block/pallas_call | solution.py:263
  20.8 5.7 %collective-permute-start.4 = (bf16[512,128]{1,0:T(8,128)(2,1)S(1)}, bf16[512,128]{1,0:T(8,128)(2,1)S(1)}, u32[]{:S(2)}, u32[]{:S(2)}) collective-permute-start(bf16[512,128]{1,0:T(8,128)(2,1)S(1)} %get-tuple-element.36), channel_id=1, source_target_pairs={{0,31},{1,0},{2,1},{3,2},{4,3},{5,4},{6,5},{7,6},{8,7},{9,8},{10,9... | collective-permute-start | bytes 393224 | tf_op jit(solution)/shard_map/ppermute | solution.py:229
  26.5 0.0 collective-permute-done.2.kv_ref.kv3_ref
  26.5 1.3 %remote_block.5 = (bf16[512,128]{1,0:T(8,128)(2,1)S(1)}, bf16[128,2048]{1,0:T(8,128)(2,1)S(1)}, bf16[128,2048]{1,0:T(8,128)(2,1)S(1)}) custom-call(s32[3]{0:T(128)S(4)} %get-tuple-element.21.half_ref, bf16[256,2048]{1,0:T(8,128)(2,1)S(1)} %get-tuple-element.22.query_ref, bf16[256,2048]{1,0:T(8,128)(2,1)S(1)} %get-tuple-element.23.grad_ref, ...), custom_call_target="tpu_custom_call" | custom-call | flops 671088640 | bytes 1048576 | tf_op jit(solution)/shard_map/remote_block/pallas_call | solution.py:263
  27.8 8.2 %collective-permute-start.5 = (bf16[512,128]{1,0:T(8,128)(2,1)S(1)}, bf16[512,128]{1,0:T(8,128)(2,1)S(1)}, u32[]{:S(2)}, u32[]{:S(2)}) collective-permute-start(bf16[512,128]{1,0:T(8,128)(2,1)S(1)} %get-tuple-element.37), channel_id=1, source_target_pairs={{0,511},{1,480},{2,481},{3,482},{4,483},{5,484},{6,485},{7,486},{8... | collective-permute-start | bytes 393224 | tf_op jit(solution)/shard_map/ppermute | solution.py:229
  36.0 3.5 %own_block.1 = (bf16[256,2048]{1,0:T(8,128)(2,1)}, f32[256,128]{1,0:T(8,128)S(1)}, f32[256,128]{1,0:T(8,128)S(1)}) custom-call(s32[3]{0:T(128)S(4)} %get-tuple-element.21.half_ref, bf16[256,2048]{1,0:T(8,128)(2,1)S(1)} %get-tuple-element.22.query_ref, bf16[256,2048]{1,0:T(8,128)(2,1)S(1)} %get-tuple-element.23.grad_ref, ...), custom_call_target="tpu_custom_call" | custom-call | flops 1342177280 | bytes 1048576 | tf_op jit(solution)/shard_map/own_block/pallas_call | solution.py:278
  39.6 0.0 collective-permute-done.3
  39.6 0.0 collective-permute-done.4
  39.6 0.0 collective-permute-done.5
  39.6 0.8 %convert_add_fusion = (f32[256,128]{1,0:T(8,128)}, f32[256,128]{1,0:T(8,128)}) fusion(f32[256,128]{1,0:T(8,128)S(1)} %get-tuple-element.38, bf16[512,128]{1,0:T(8,128)(2,1)S(1)} %collective-permute-done.5, bf16[512,128]{1,0:T(8,128)(2,1)S(1)} %collective-permute-done.4, bf16[512,128]{1,0:T(8,128)(2,1)S(1)} %collective-permute-done.3, ...), kind=kLoop, calls=%fused_computation | loop fusion | flops 425984 | bytes 917504 | tf_op jit(solution)/shard_map/add | solution.py:296
Async XLA Ops:
  3.0 11.5 %collective-permute-start = (bf16[512,128]{1,0:T(8,128)(2,1)S(1)}, bf16[512,128]{1,0:T(8,128)(2,1)S(1)}, u32[]{:S(2)}, u32[]{:S(2)}) collective-permute-start(bf16[512,128]{1,0:T(8,128)(2,1)S(1)} %get-tuple-element.24.kv_ref), channel_id=1, source_target_pairs={{0,32},{1,33},{2,34},{3,35},{4,36},{5,37},{6,38},{7,39},{8,40},{9,... | collective-permute-start | bytes 393224 | tf_op jit(solution)/shard_map/ppermute | solution.py:229
  7.0 12.4 %collective-permute-start.1 = (bf16[512,128]{1,0:T(8,128)(2,1)S(1)}, bf16[512,128]{1,0:T(8,128)(2,1)S(1)}, u32[]{:S(2)}, u32[]{:S(2)}) collective-permute-start(bf16[512,128]{1,0:T(8,128)(2,1)S(1)} %get-tuple-element.24.kv_ref), channel_id=1, source_target_pairs={{0,1},{1,2},{2,3},{3,4},{4,5},{5,6},{6,7},{7,8},{8,9},{9,10},{10,1... | collective-permute-start | bytes 393224 | tf_op jit(solution)/shard_map/ppermute | solution.py:229
  12.2 14.3 %collective-permute-start.2 = (bf16[512,128]{1,0:T(8,128)(2,1)S(1)}, bf16[512,128]{1,0:T(8,128)(2,1)S(1)}, u32[]{:S(2)}, u32[]{:S(2)}) collective-permute-start(bf16[512,128]{1,0:T(8,128)(2,1)S(1)} %get-tuple-element.24.kv_ref), channel_id=1, source_target_pairs={{0,33},{1,34},{2,35},{3,36},{4,37},{5,38},{6,39},{7,40},{8,41},{9,... | collective-permute-start | bytes 393224 | tf_op jit(solution)/shard_map/ppermute | solution.py:229
  15.8 23.7 %collective-permute-start.3 = (bf16[512,128]{1,0:T(8,128)(2,1)S(1)}, bf16[512,128]{1,0:T(8,128)(2,1)S(1)}, u32[]{:S(2)}, u32[]{:S(2)}) collective-permute-start(bf16[512,128]{1,0:T(8,128)(2,1)S(1)} %get-tuple-element.35), channel_id=1, source_target_pairs={{0,480},{1,481},{2,482},{3,483},{4,484},{5,485},{6,486},{7,487},{8... | collective-permute-start | bytes 393224 | tf_op jit(solution)/shard_map/ppermute | solution.py:229
  20.8 18.8 %collective-permute-start.4 = (bf16[512,128]{1,0:T(8,128)(2,1)S(1)}, bf16[512,128]{1,0:T(8,128)(2,1)S(1)}, u32[]{:S(2)}, u32[]{:S(2)}) collective-permute-start(bf16[512,128]{1,0:T(8,128)(2,1)S(1)} %get-tuple-element.36), channel_id=1, source_target_pairs={{0,31},{1,0},{2,1},{3,2},{4,3},{5,4},{6,5},{7,6},{8,7},{9,8},{10,9... | collective-permute-start | bytes 393224 | tf_op jit(solution)/shard_map/ppermute | solution.py:229
  27.8 11.8 %collective-permute-start.5 = (bf16[512,128]{1,0:T(8,128)(2,1)S(1)}, bf16[512,128]{1,0:T(8,128)(2,1)S(1)}, u32[]{:S(2)}, u32[]{:S(2)}) collective-permute-start(bf16[512,128]{1,0:T(8,128)(2,1)S(1)} %get-tuple-element.37), channel_id=1, source_target_pairs={{0,511},{1,480},{2,481},{3,482},{4,483},{5,484},{6,485},{7,486},{8... | collective-permute-start | bytes 393224 | tf_op jit(solution)/shard_map/ppermute | solution.py:229

commit v3 on v2

v3 whole, which is shorter than its diff:
```python
import functools
import math

import jax
import jax.numpy as jnp
from jax import lax
from jax.experimental import pallas as pl
from jax.experimental.pallas import tpu as pltpu
from jax.sharding import PartitionSpec as P

F32 = jnp.float32
BF16 = jnp.bfloat16
HEADS = 16
HD = 128
SPAN = 128
WIDE = HEADS * HD
FACTOR = 1.0 / math.sqrt(HD)
OUTER = 16
INNER = 32
STEPS = ((1, 0), (1, 1), (0, 1))
EARLY = 4
LOG2E = math.log2(math.e)


def dot(a, b, contract):
    return lax.dot_general(a, b, ((contract[:1], contract[1:]), ((), ())), preferred_element_type=F32)


def stacked(ref, rows):
    return jnp.concatenate([ref[rows, h * HD : (h + 1) * HD] for h in range(HEADS)], 0)


def sub_block(key, value, query_ref, grad_ref, rows, log_two, row_dot, mask=None, ready=None):
    probs, dscores = [], []
    for m in range(0, HEADS, 2):
        if ready is not None:
            ready(m)
        one, two = slice(m * HD, (m + 1) * HD), slice((m + 1) * HD, (m + 2) * HD)
        pair = jnp.concatenate([query_ref[rows, one], query_ref[rows, two]], 0)
        grad = jnp.concatenate([grad_ref[rows, one], grad_ref[rows, two]], 0)
        lanes = lambda of: jnp.concatenate([of(m), of(m + 1)], 1)
        scores = dot(key, pair, (1, 1))
        weights = jnp.exp2(scores * (FACTOR * LOG2E) - lanes(log_two))
        if mask is not None:
            weights = jnp.where(mask, weights, 0.0)
        dweights = dot(value, grad, (1, 1))
        probs.append(weights.astype(BF16))
        dscores.append((weights * (dweights - lanes(row_dot))).astype(BF16))
    return jnp.concatenate(probs, 1), jnp.concatenate(dscores, 1)


def of_rows(ref, rows):
    return lambda h: ref[h : h + 1, rows]


def of_half(ref, is_low):
    return lambda h: jnp.where(is_low, ref[h : h + 1, 0:SPAN], ref[h : h + 1, SPAN:])


def pack_kernel(place_ref, table_hbm, key_hbm, value_hbm, packed_ref, plan_ref, table_ref, sems):
    rows = 2 * SPAN
    copies = [
        pltpu.make_async_copy(table_hbm, table_ref, sems.at[0]),
        pltpu.make_async_copy(key_hbm, packed_ref.at[0:rows], sems.at[1]),
        pltpu.make_async_copy(value_hbm, packed_ref.at[rows : 2 * rows], sems.at[2]),
    ]
    for copy in copies:
        copy.start()
    outer, inner = place_ref[0] // INNER, place_ref[0] % INNER
    plan_ref[len(STEPS)] = (inner < EARLY).astype(jnp.int32)
    copies[0].wait()
    own = table_ref[0, outer * INNER + inner]
    for j, (a, b) in enumerate(STEPS):
        source = (outer - a + OUTER) % OUTER * INNER + (inner - b + INNER) % INNER
        plan_ref[j] = (table_ref[0, source] > own).astype(jnp.int32)
    copies[1].wait()
    copies[2].wait()


def load_kernel(
    plan_ref,
    query_hbm,
    grad_hbm,
    out_hbm,
    sum_hbm,
    kv_ref,
    query_ref,
    grad_ref,
    log_ref,
    dot_ref,
    own_scores_ref,
    key_grad_ref,
    value_grad_ref,
    out_ref,
    sum_ref,
    sems,
):
    first = pltpu.make_async_copy(sum_hbm, sum_ref, sems.at[0])
    first.start()
    halves = (slice(0, SPAN), slice(SPAN, 2 * SPAN))
    pairs = ((grad_hbm, grad_ref), (out_hbm, out_ref), (query_hbm, query_ref))
    copies = [[pltpu.make_async_copy(a.at[r], b.at[r], sems.at[1 + 2 * i + n]) for n, r in enumerate(halves)] for i, (a, b) in enumerate(pairs)]
    for n in range(2):
        copies[0][n].start()
        copies[1][n].start()
    for n in range(2):
        copies[2][n].start()
    first.wait()
    log_ref[...] = sum_ref[...] * LOG2E
    for n, r in enumerate(halves):
        copies[0][n].wait()
        copies[1][n].wait()
        dot_ref[:, r] = row_dots(grad_ref, out_ref, r)
    for n in range(2):
        copies[2][n].wait()

    @pl.when(plan_ref[len(STEPS)] != 0)
    def _():
        own_block(query_ref, grad_ref, kv_ref, log_ref, dot_ref, own_scores_ref, key_grad_ref, value_grad_ref)


def own_block(query_ref, grad_ref, kv_ref, log_ref, dot_ref, scores_ref, key_grad_ref, value_grad_ref):
    low, high = slice(0, SPAN), slice(SPAN, 2 * SPAN)
    span = (SPAN, 2 * SPAN)
    keys = lax.broadcasted_iota(jnp.int32, span, 0)
    mask = keys <= lax.rem(lax.broadcasted_iota(jnp.int32, span, 1), SPAN)
    key_low, key_high = kv_ref[low, :], kv_ref[high, :]
    value_low, value_high = kv_ref[2 * SPAN : 3 * SPAN, :], kv_ref[3 * SPAN :, :]

    def block(n, key, value, rows, mask=None):
        probs, dscores = sub_block(
            key, value, query_ref, grad_ref, rows, of_rows(log_ref, rows), of_rows(dot_ref, rows), mask
        )
        scores_ref[n * SPAN : (n + 1) * SPAN, :] = dscores
        return dot(dscores, stacked(query_ref, rows), (1, 0)), dot(probs, stacked(grad_ref, rows), (1, 0))

    key_ll, value_ll = block(0, key_low, value_low, low, mask)
    key_lh, value_lh = block(1, key_low, value_low, high)
    key_hh, value_hh = block(2, key_high, value_high, high, mask)
    key_grad_ref[low, :] = key_ll + key_lh
    key_grad_ref[high, :] = key_hh
    value_grad_ref[low, :] = value_ll + value_lh
    value_grad_ref[high, :] = value_hh


def row_dots(grad_ref, out_ref, rows):
    columns = []
    for h in range(HEADS):
        one = slice(h * HD, (h + 1) * HD)
        product = grad_ref[rows, one].astype(F32) * out_ref[rows, one].astype(F32)
        columns.append(jnp.sum(product, axis=1, keepdims=True))
    return jnp.concatenate(columns, 1).T


def remote_low(query_ref, grad_ref, kv_refs, log_ref, dot_ref, scores_ref):
    high = slice(SPAN, 2 * SPAN)
    key = jnp.concatenate([ref[0:SPAN, :] for ref in kv_refs], 0)
    value = jnp.concatenate([ref[2 * SPAN : 3 * SPAN, :] for ref in kv_refs], 0)
    probs, dscores = sub_block(key, value, query_ref, grad_ref, high, of_rows(log_ref, high), of_rows(dot_ref, high))
    scores_ref[...] = dscores
    return dot(dscores, stacked(query_ref, high), (1, 0)), dot(probs, stacked(grad_ref, high), (1, 0))


def remote_half(half, query_ref, grad_ref, kv_ref, log_ref, dot_ref, scores_ref, key_low, value_low):
    rows = pl.ds(pl.multiple_of(half * SPAN, SPAN), SPAN)
    is_low = half == 0
    key, value = kv_ref[rows, :], kv_ref[pl.ds(pl.multiple_of((half + 2) * SPAN, SPAN), SPAN), :]
    probs, dscores = sub_block(
        key, value, query_ref, grad_ref, rows, of_half(log_ref, is_low), of_half(dot_ref, is_low)
    )
    scores_ref[...] = dscores
    key_half = dot(dscores, stacked(query_ref, rows), (1, 0))
    value_half = dot(probs, stacked(grad_ref, rows), (1, 0))
    return jnp.concatenate(
        [
            key_low + jnp.where(is_low, key_half, 0.0),
            jnp.where(is_low, 0.0, key_half),
            value_low + jnp.where(is_low, value_half, 0.0),
            jnp.where(is_low, 0.0, value_half),
        ],
        0,
    )


def outer_kernel(plan_ref, query_ref, grad_ref, kv_ref, log_ref, dot_ref, part_ref, low_ref, half_ref):
    key_low, value_low = remote_low(query_ref, grad_ref, (kv_ref,), log_ref, dot_ref, low_ref)
    part_ref[...] = remote_half(
        plan_ref[0], query_ref, grad_ref, kv_ref, log_ref, dot_ref, half_ref, key_low, value_low
    ).astype(BF16)


def inner_kernel(
    plan_ref, query_ref, grad_ref, kv1_ref, kv2_ref, log_ref, dot_ref, part1_ref, part2_ref, low_ref, half_ref
):
    key_low, value_low = remote_low(query_ref, grad_ref, (kv1_ref, kv2_ref), log_ref, dot_ref, low_ref)
    for j, (kv_ref, part_ref) in enumerate(((kv1_ref, part1_ref), (kv2_ref, part2_ref))):
        rows = slice(j * SPAN, (j + 1) * SPAN)
        part_ref[...] = remote_half(
            plan_ref[1 + j],
            query_ref,
            grad_ref,
            kv_ref,
            log_ref,
            dot_ref,
            half_ref.at[rows],
            key_low[rows],
            value_low[rows],
        ).astype(BF16)


def last_kernel(
    plan_ref,
    query_ref,
    grad_ref,
    kv_ref,
    log_ref,
    dot_ref,
    kv1_ref,
    kv2_ref,
    kv3_ref,
    low1_ref,
    half1_ref,
    low23_ref,
    half23_ref,
    _own_scores,
    _key_grad,
    _value_grad,
    query_grad_hbm,
    scores_ref,
    key_grad_ref,
    value_grad_ref,
    query_grad_ref,
    sems,
):
    @pl.when(plan_ref[len(STEPS)] == 0)
    def _():
        own_block(query_ref, grad_ref, kv_ref, log_ref, dot_ref, scores_ref, key_grad_ref, value_grad_ref)

    low, high = slice(0, SPAN), slice(SPAN, 2 * SPAN)
    zero = jnp.zeros((SPAN, HD), BF16)
    remotes = (
        (kv1_ref, low1_ref, half1_ref),
        (kv2_ref, low23_ref.at[low], half23_ref.at[low]),
        (kv3_ref, low23_ref.at[high], half23_ref.at[high]),
    )

    def query_part(n, rows, keys, scores):
        total = dot(jnp.concatenate(keys, 0).T, jnp.concatenate(scores, 0), (1, 0)) * FACTOR
        for h in range(HEADS):
            one = slice(h * HD, (h + 1) * HD)
            query_grad_ref[rows, one] = total[:, one].T.astype(BF16)
        copy = pltpu.make_async_copy(query_grad_ref.at[rows], query_grad_hbm.at[rows], sems.at[n])
        copy.start()
        return copy

    keys, scores = [kv_ref[low, :], kv_ref[high, :]], [scores_ref[SPAN : 2 * SPAN, :], scores_ref[2 * SPAN :, :]]
    for j, (ref, first, second) in enumerate(remotes):
        keys += [ref[low, :], jnp.where(plan_ref[j] == 0, zero, ref[high, :])]
        scores += [first[...], second[...]]
    copy_high = query_part(1, high, keys, scores)
    keys, scores = [kv_ref[low, :]], [scores_ref[low, :]]
    for j, (ref, first, second) in enumerate(remotes):
        keys.append(jnp.where(plan_ref[j] == 0, ref[low, :], zero))
        scores.append(second[...])
    copy_low = query_part(0, low, keys, scores)
    copy_high.wait()
    copy_low.wait()


VMEM = pl.BlockSpec(memory_space=pltpu.VMEM)
ANY = pl.BlockSpec(memory_space=pl.ANY)
SMEM = pl.BlockSpec(memory_space=pltpu.SMEM)
PARAMS = pltpu.CompilerParams(vmem_limit_bytes=24 << 20)


def units(count):
    return pl.CostEstimate(flops=count * 10 * SPAN * HD * SPAN * HEADS, bytes_accessed=1 << 20, transcendentals=count * SPAN * SPAN * HEADS)


def shifted(shard, by_outer, by_inner):
    outer, inner = lax.axis_size("outer"), lax.axis_size("inner")
    pairs = [
        (o * inner + i, (o + by_outer) % outer * inner + (i + by_inner) % inner) for o in range(outer) for i in range(inner)
    ]
    return lax.ppermute(shard, ("outer", "inner"), pairs)


def per_device(queries, key_rows, value_rows, out_grad, outputs, log_sum, span_table):
    rows = 2 * SPAN
    place = lax.axis_index(("outer", "inner")).reshape(1)
    table, key_rows, value_rows, queries, out_grad, outputs, log_sum = (
        pltpu.with_memory_space_constraint(x, pltpu.HBM)
        for x in (span_table.T, key_rows, value_rows, queries, out_grad, outputs, log_sum)
    )
    packed, plan = pl.pallas_call(
        pack_kernel,
        out_shape=(pltpu.VMEM((2 * rows, HD), BF16), pltpu.SMEM((len(STEPS) + 1,), jnp.int32)),
        in_specs=[SMEM] + [ANY] * 3,
        out_specs=(VMEM, SMEM),
        scratch_shapes=[pltpu.SMEM((2, OUTER * INNER), jnp.int32), pltpu.SemaphoreType.DMA((3,))],
        compiler_params=PARAMS,
        name="pack",
    )(place, table, key_rows, value_rows)
    arrived = [shifted(packed, a, b) for a, b in STEPS]
    wide = pltpu.VMEM((rows, WIDE), BF16)
    small = pltpu.VMEM((HEADS, rows), F32)
    part = pltpu.VMEM((2 * rows, HD), BF16)
    total = pltpu.VMEM((rows, HD), F32)

    def spans(count):
        return pltpu.VMEM((count * SPAN, WIDE), BF16)

    queries, out_grad, log_two, row_dot, own_scores, key_own, value_own = pl.pallas_call(
        load_kernel,
        out_shape=(wide, wide, small, small, spans(3), total, total),
        in_specs=[SMEM] + [ANY] * 4 + [VMEM],
        out_specs=(VMEM,) * 7,
        scratch_shapes=[wide, small, pltpu.SemaphoreType.DMA((7,))],
        compiler_params=PARAMS,
        cost_estimate=units(2),
        name="load",
    )(plan, queries, out_grad, outputs, log_sum, packed)
    part1, low1, half1 = pl.pallas_call(
        outer_kernel,
        out_shape=(part, spans(1), spans(1)),
        in_specs=[SMEM] + [VMEM] * 5,
        out_specs=(VMEM,) * 3,
        compiler_params=PARAMS,
        cost_estimate=units(2),
        name="outer_block",
    )(plan, queries, out_grad, arrived[0], log_two, row_dot)
    back = [shifted(part1, -1, 0)]
    part2, part3, low23, half23 = pl.pallas_call(
        inner_kernel,
        out_shape=(part, part, spans(2), spans(2)),
        in_specs=[SMEM] + [VMEM] * 6,
        out_specs=(VMEM,) * 4,
        compiler_params=PARAMS,
        cost_estimate=units(4),
        name="inner_blocks",
    )(plan, queries, out_grad, arrived[1], arrived[2], log_two, row_dot)
    back += [shifted(part2, -1, -1), shifted(part3, 0, -1)]
    query_grad, _, key_total, value_total = pl.pallas_call(
        last_kernel,
        out_shape=(pltpu.HBM((rows, WIDE), BF16), spans(3), total, total),
        in_specs=[SMEM] + [VMEM] * 15,
        out_specs=(ANY, VMEM, VMEM, VMEM),
        scratch_shapes=[wide, pltpu.SemaphoreType.DMA((2,))],
        input_output_aliases={13: 1, 14: 2, 15: 3},
        compiler_params=PARAMS,
        cost_estimate=units(4),
        name="last",
    )(
        plan,
        queries,
        out_grad,
        packed,
        log_two,
        row_dot,
        *arrived,
        low1,
        half1,
        low23,
        half23,
        own_scores,
        key_own,
        value_own,
    )
    for one in back:
        key_total = key_total + one[:rows].astype(F32)
        value_total = value_total + one[rows:].astype(F32)
    return (query_grad, key_total * FACTOR, value_total)


def solution(mesh):
    tokens = P(("outer", "inner"), None)
    return jax.shard_map(
        per_device,
        mesh=mesh,
        in_specs=(tokens,) * 5 + (P(None, ("outer", "inner")), P()),
        out_specs=(tokens,) * 3,
        check_vma=False,
    )
```

time: 40.6 us -> 39.5 us (0.973)
  starting transfers between devices: 28.9 us -> 26 us
  waiting for transfers between devices: 0.02 us -> 0.89 us
  Pallas kernels: 9.87 us -> 10.7 us
    ppermute x6, starting transfers between devices: 28.9 us -> 26 us  [shifted(): return lax.ppermute(shard, ('outer', 'inner'), pairs)]
    pallas_call x4, Pallas kernels: 7.5 us -> 9.77 us  [the longest x1 4.04 us: per_device(): pl.pallas_call(load_kernel, out_shape=(wide, wide, small, small, spans(3)...]
    pallas_call x1, Pallas kernels: 2.37 us -> 0.9 us  [per_device(): pl.pallas_call(pack_kernel, out_shape=(pltpu.VMEM((2 * rows, HD), BF16),...]
    ppermute x6, waiting for transfers between devices: 0.02 us -> 0.89 us  [shifted(): return lax.ppermute(shard, ('outer', 'inner'), pairs)]
  transfers between devices with their start and end apart: 6 -> 6, of which waited for: 0 -> 1; matrix products, arithmetic and copies ran while one was open for 0% -> 0% of each run, Pallas kernels for 19% -> 25%
where the time goes in v3:
time: 39.5 us; the launch traced here: 39.1 us
  starting transfers between devices  26 us (66%)
  Pallas kernels  10.7 us (27%)
  waiting for transfers between devices  0.89 us (2%)
  other arithmetic  0.76 us (2%)
  between operations  0.76 us (2%)
    ppermute x6, starting transfers between devices, shifted(): return lax.ppermute(shard, ('outer', 'inner'), pairs)  26 us
    pallas_call x1, Pallas kernels, per_device(): pl.pallas_call(load_kernel, out_shape=(wide, wide, small, small, spans(3)...  4.04 us
    pallas_call x1, Pallas kernels, per_device(): pl.pallas_call(inner_kernel, out_shape=(part, part, spans(2), spans(2)),...  2.48 us
    pallas_call x1, Pallas kernels, per_device(): pl.pallas_call(last_kernel, out_shape=(pltpu.HBM((rows, WIDE), BF16), spa...  1.93 us
    pallas_call x1, Pallas kernels, per_device(): pl.pallas_call(outer_kernel, out_shape=(part, spans(1), spans(1)), in_spe...  1.32 us
    pallas_call x1, Pallas kernels, per_device(): pl.pallas_call(pack_kernel, out_shape=(pltpu.VMEM((2 * rows, HD), BF16),...  0.9 us
    ppermute x6, waiting for transfers between devices, shifted(): return lax.ppermute(shard, ('outer', 'inner'), pairs)  0.89 us
  transfers between devices with their start and end apart: 6, of which 1 were waited for; matrix products, arithmetic and copies ran while one was open for 0% of the time, Pallas kernels for 25%

profile of v3, /device:TPU:1, one launch (start us, length us, event | category | flops | bytes accessed | tf_op | source)
XLA Modules:
  0.0 39.1 jit_solution(16397624134318082083)
XLA Ops:
  0.6 0.9 %pack.1 = (bf16[512,128]{1,0:T(8,128)(2,1)S(1)}, s32[4]{0:T(128)S(4)}) custom-call(s32[1]{0:T(128)} %bitcast.place_ref, s32[2,512]{1,0:T(2,128)} %bitcast.2, bf16[256,128]{1,0:T(8,128)(2,1)} %key_hbm.1, bf16[256,128]{1,0:T(8,128)(2,1)} %value_hbm.1), custom_call_target="tpu_custom_call" | custom-call | tf_op jit(solution)/shard_map/pack/pallas_call | solution.py:295
  1.5 3.9 %collective-permute-start = (bf16[512,128]{1,0:T(8,128)(2,1)S(1)}, bf16[512,128]{1,0:T(8,128)(2,1)S(1)}, u32[]{:S(2)}, u32[]{:S(2)}) collective-permute-start(bf16[512,128]{1,0:T(8,128)(2,1)S(1)} %get-tuple-element.23.kv_ref), channel_id=1, source_target_pairs={{0,32},{1,33},{2,34},{3,35},{4,36},{5,37},{6,38},{7,39},{8,40},{9,... | collective-permute-start | bytes 393224 | tf_op jit(solution)/shard_map/ppermute | solution.py:285
  5.5 5.2 %collective-permute-start.2 = (bf16[512,128]{1,0:T(8,128)(2,1)S(1)}, bf16[512,128]{1,0:T(8,128)(2,1)S(1)}, u32[]{:S(2)}, u32[]{:S(2)}) collective-permute-start(bf16[512,128]{1,0:T(8,128)(2,1)S(1)} %get-tuple-element.23.kv_ref), channel_id=1, source_target_pairs={{0,1},{1,2},{2,3},{3,4},{4,5},{5,6},{6,7},{7,8},{8,9},{9,10},{10,1... | collective-permute-start | bytes 393224 | tf_op jit(solution)/shard_map/ppermute | solution.py:285
  10.7 2.3 %collective-permute-start.1 = (bf16[512,128]{1,0:T(8,128)(2,1)S(1)}, bf16[512,128]{1,0:T(8,128)(2,1)S(1)}, u32[]{:S(2)}, u32[]{:S(2)}) collective-permute-start(bf16[512,128]{1,0:T(8,128)(2,1)S(1)} %get-tuple-element.23.kv_ref), channel_id=1, source_target_pairs={{0,33},{1,34},{2,35},{3,36},{4,37},{5,38},{6,39},{7,40},{8,41},{9,... | collective-permute-start | bytes 393224 | tf_op jit(solution)/shard_map/ppermute | solution.py:285
  13.0 4.0 %load.1 = (bf16[256,2048]{1,0:T(8,128)(2,1)S(1)}, bf16[256,2048]{1,0:T(8,128)(2,1)S(1)}, f32[16,256]{1,0:T(8,128)S(1)}, f32[16,256]{1,0:T(8,128)S(1)}, bf16[384,...) custom-call(s32[4]{0:T(128)S(4)} %get-tuple-element.22.plan_ref, ...), custom_call_target="tpu_custom_call" | custom-call | flops 671088640 | bytes 1048576 | tf_op jit(solution)/shard_map/load/pallas_call | solution.py:313
  17.1 0.0 collective-permute-done.kv_ref.kv1_ref
  17.1 1.3 %outer_block.1 = (bf16[512,128]{1,0:T(8,128)(2,1)S(1)}, bf16[128,2048]{1,0:T(8,128)(2,1)S(1)}, bf16[128,2048]{1,0:T(8,128)(2,1)S(1)}) custom-call(s32[4]{0:T(128)S(4)} %get-tuple-element.22.plan_ref, bf16[256,2048]{1,0:T(8,128)(2,1)S(1)} %get-tuple-element.24.query_ref, bf16[256,2048]{1,0:T(8,128)(2,1)S(1)} %get-tuple-element.25.grad_ref, ...), custom_call_target="tpu_custom_call" | custom-call | flops 671088640 | bytes 1048576 | tf_op jit(solution)/shard_map/outer_block/pallas_call | solution.py:323
  18.4 3.6 %collective-permute-start.3 = (bf16[512,128]{1,0:T(8,128)(2,1)S(1)}, bf16[512,128]{1,0:T(8,128)(2,1)S(1)}, u32[]{:S(2)}, u32[]{:S(2)}) collective-permute-start(bf16[512,128]{1,0:T(8,128)(2,1)S(1)} %get-tuple-element.37), channel_id=1, source_target_pairs={{0,480},{1,481},{2,482},{3,483},{4,484},{5,485},{6,486},{7,487},{8... | collective-permute-start | bytes 393224 | tf_op jit(solution)/shard_map/ppermute | solution.py:285
  22.0 0.0 collective-permute-done.2.kv2_ref.kv3_ref
  22.0 0.0 collective-permute-done.1.kv1_ref.kv2_ref
  22.0 2.5 %inner_blocks.1 = (bf16[512,128]{1,0:T(8,128)(2,1)S(1)}, bf16[512,128]{1,0:T(8,128)(2,1)S(1)}, bf16[256,2048]{1,0:T(8,128)(2,1)S(1)}, bf16[256,2048]{1,0:T(8,128)(2,1)S(1)}) custom-call(s32[4]{0:T(128)S(4)} %get-tuple-element.22.plan_ref, bf16[256,2048]{1,0:T(8,128)(2,1)S(1)} %get-tuple-element.24.query_ref, ...), custom_call_target="tpu_custom_call" | custom-call | flops 1342177280 | bytes 1048576 | tf_op jit(solution)/shard_map/inner_blocks/pallas_call | solution.py:333
  24.5 6.1 %collective-permute-start.4 = (bf16[512,128]{1,0:T(8,128)(2,1)S(1)}, bf16[512,128]{1,0:T(8,128)(2,1)S(1)}, u32[]{:S(2)}, u32[]{:S(2)}) collective-permute-start(bf16[512,128]{1,0:T(8,128)(2,1)S(1)} %get-tuple-element.38), channel_id=1, source_target_pairs={{0,511},{1,480},{2,481},{3,482},{4,483},{5,484},{6,485},{7,486},{8... | collective-permute-start | bytes 393224 | tf_op jit(solution)/shard_map/ppermute | solution.py:285
  30.6 5.0 %collective-permute-start.5 = (bf16[512,128]{1,0:T(8,128)(2,1)S(1)}, bf16[512,128]{1,0:T(8,128)(2,1)S(1)}, u32[]{:S(2)}, u32[]{:S(2)}) collective-permute-start(bf16[512,128]{1,0:T(8,128)(2,1)S(1)} %get-tuple-element.39), channel_id=1, source_target_pairs={{0,31},{1,0},{2,1},{3,2},{4,3},{5,4},{6,5},{7,6},{8,7},{9,8},{10,9... | collective-permute-start | bytes 393224 | tf_op jit(solution)/shard_map/ppermute | solution.py:285
  35.5 1.9 %last.1 = (bf16[256,2048]{1,0:T(8,128)(2,1)}, bf16[384,2048]{1,0:T(8,128)(2,1)S(1)}, f32[256,128]{1,0:T(8,128)S(1)}, f32[256,128]{1,0:T(8,128)S(1)}) custom-call(s32[4]{0:T(128)S(4)} %get-tuple-element.22.plan_ref, bf16[256,2048]{1,0:T(8,128)(2,1)S(1)} %get-tuple-element.24.query_ref, ...), custom_call_target="tpu_custom_call", output_to_operand_aliasing={{1}: (13, {}), {2}: (14, {}), {3}: (15, {})} | custom-call | flops 1342177280 | bytes 1048576 | tf_op jit(solution)/shard_map/last/pallas_call | solution.py:343
  37.5 0.0 collective-permute-done.3
  37.5 0.0 collective-permute-done.4
  37.5 0.9 %collective-permute-done.5 = bf16[512,128]{1,0:T(8,128)(2,1)S(1)} collective-permute-done((bf16[512,128]{1,0:T(8,128)(2,1)S(1)}, bf16[512,128]{1,0:T(8,128)(2,1)S(1)}, u32[]{:S(2)}, u32[]{:S(2)}) %collective-permute-start.5) | collective-permute-done | bytes 131104 | tf_op jit(solution)/shard_map/ppermute | solution.py:285
  38.4 0.8 %convert_add_fusion = (f32[256,128]{1,0:T(8,128)}, f32[256,128]{1,0:T(8,128)}) fusion(f32[256,128]{1,0:T(8,128)S(1)} %get-tuple-element.40, bf16[512,128]{1,0:T(8,128)(2,1)S(1)} %collective-permute-done.5, bf16[512,128]{1,0:T(8,128)(2,1)S(1)} %collective-permute-done.4, bf16[512,128]{1,0:T(8,128)(2,1)S(1)} %collective-permute-done.3, ...), kind=kLoop, calls=%fused_computation | loop fusion | flops 425984 | bytes 917504 | tf_op jit(solution)/shard_map/add | solution.py:371
Async XLA Ops:
  1.5 15.5 %collective-permute-start = (bf16[512,128]{1,0:T(8,128)(2,1)S(1)}, bf16[512,128]{1,0:T(8,128)(2,1)S(1)}, u32[]{:S(2)}, u32[]{:S(2)}) collective-permute-start(bf16[512,128]{1,0:T(8,128)(2,1)S(1)} %get-tuple-element.23.kv_ref), channel_id=1, source_target_pairs={{0,32},{1,33},{2,34},{3,35},{4,36},{5,37},{6,38},{7,39},{8,40},{9,... | collective-permute-start | bytes 393224 | tf_op jit(solution)/shard_map/ppermute | solution.py:285
  5.5 16.5 %collective-permute-start.2 = (bf16[512,128]{1,0:T(8,128)(2,1)S(1)}, bf16[512,128]{1,0:T(8,128)(2,1)S(1)}, u32[]{:S(2)}, u32[]{:S(2)}) collective-permute-start(bf16[512,128]{1,0:T(8,128)(2,1)S(1)} %get-tuple-element.23.kv_ref), channel_id=1, source_target_pairs={{0,1},{1,2},{2,3},{3,4},{4,5},{5,6},{6,7},{7,8},{8,9},{9,10},{10,1... | collective-permute-start | bytes 393224 | tf_op jit(solution)/shard_map/ppermute | solution.py:285
  10.7 11.3 %collective-permute-start.1 = (bf16[512,128]{1,0:T(8,128)(2,1)S(1)}, bf16[512,128]{1,0:T(8,128)(2,1)S(1)}, u32[]{:S(2)}, u32[]{:S(2)}) collective-permute-start(bf16[512,128]{1,0:T(8,128)(2,1)S(1)} %get-tuple-element.23.kv_ref), channel_id=1, source_target_pairs={{0,33},{1,34},{2,35},{3,36},{4,37},{5,38},{6,39},{7,40},{8,41},{9,... | collective-permute-start | bytes 393224 | tf_op jit(solution)/shard_map/ppermute | solution.py:285
  18.4 19.1 %collective-permute-start.3 = (bf16[512,128]{1,0:T(8,128)(2,1)S(1)}, bf16[512,128]{1,0:T(8,128)(2,1)S(1)}, u32[]{:S(2)}, u32[]{:S(2)}) collective-permute-start(bf16[512,128]{1,0:T(8,128)(2,1)S(1)} %get-tuple-element.37), channel_id=1, source_target_pairs={{0,480},{1,481},{2,482},{3,483},{4,484},{5,485},{6,486},{7,487},{8... | collective-permute-start | bytes 393224 | tf_op jit(solution)/shard_map/ppermute | solution.py:285
  24.5 13.0 %collective-permute-start.4 = (bf16[512,128]{1,0:T(8,128)(2,1)S(1)}, bf16[512,128]{1,0:T(8,128)(2,1)S(1)}, u32[]{:S(2)}, u32[]{:S(2)}) collective-permute-start(bf16[512,128]{1,0:T(8,128)(2,1)S(1)} %get-tuple-element.38), channel_id=1, source_target_pairs={{0,511},{1,480},{2,481},{3,482},{4,483},{5,484},{6,485},{7,486},{8... | collective-permute-start | bytes 393224 | tf_op jit(solution)/shard_map/ppermute | solution.py:285
  30.6 7.8 %collective-permute-start.5 = (bf16[512,128]{1,0:T(8,128)(2,1)S(1)}, bf16[512,128]{1,0:T(8,128)(2,1)S(1)}, u32[]{:S(2)}, u32[]{:S(2)}) collective-permute-start(bf16[512,128]{1,0:T(8,128)(2,1)S(1)} %get-tuple-element.39), channel_id=1, source_target_pairs={{0,31},{1,0},{2,1},{3,2},{4,3},{5,4},{6,5},{7,6},{8,7},{9,8},{10,9... | collective-permute-start | bytes 393224 | tf_op jit(solution)/shard_map/ppermute | solution.py:285

commit v4 on v3

--- a/solution.py
+++ b/solution.py
@@ -17,7 +17,7 @@
 FACTOR = 1.0 / math.sqrt(HD)
 OUTER = 16
 INNER = 32
-STEPS = ((1, 0), (1, 1), (0, 1))
+STEPS = ((1, 0), (0, 1), (1, 1))
 EARLY = 4
 LOG2E = math.log2(math.e)
 
@@ -78,41 +78,10 @@
 
 
 def load_kernel(
-    plan_ref,
-    query_hbm,
-    grad_hbm,
-    out_hbm,
-    sum_hbm,
-    kv_ref,
-    query_ref,
-    grad_ref,
-    log_ref,
-    dot_ref,
-    own_scores_ref,
-    key_grad_ref,
-    value_grad_ref,
-    out_ref,
-    sum_ref,
-    sems,
+    plan_ref, query_ref, grad_ref, out_ref, sum_ref, kv_ref, log_ref, dot_ref, own_scores_ref, key_grad_ref, value_grad_ref
 ):
-    first = pltpu.make_async_copy(sum_hbm, sum_ref, sems.at[0])
-    first.start()
-    halves = (slice(0, SPAN), slice(SPAN, 2 * SPAN))
-    pairs = ((grad_hbm, grad_ref), (out_hbm, out_ref), (query_hbm, query_ref))
-    copies = [[pltpu.make_async_copy(a.at[r], b.at[r], sems.at[1 + 2 * i + n]) for n, r in enumerate(halves)] for i, (a, b) in enumerate(pairs)]
-    for n in range(2):
-        copies[0][n].start()
-        copies[1][n].start()
-    for n in range(2):
-        copies[2][n].start()
-    first.wait()
     log_ref[...] = sum_ref[...] * LOG2E
-    for n, r in enumerate(halves):
-        copies[0][n].wait()
-        copies[1][n].wait()
-        dot_ref[:, r] = row_dots(grad_ref, out_ref, r)
-    for n in range(2):
-        copies[2][n].wait()
+    dot_ref[...] = row_dots(grad_ref, out_ref, slice(0, 2 * SPAN))
 
     @pl.when(plan_ref[len(STEPS)] != 0)
     def _():
@@ -152,10 +121,9 @@
     return jnp.concatenate(columns, 1).T
 
 
-def remote_low(query_ref, grad_ref, kv_refs, log_ref, dot_ref, scores_ref):
+def remote_low(query_ref, grad_ref, kv_ref, log_ref, dot_ref, scores_ref):
     high = slice(SPAN, 2 * SPAN)
-    key = jnp.concatenate([ref[0:SPAN, :] for ref in kv_refs], 0)
-    value = jnp.concatenate([ref[2 * SPAN : 3 * SPAN, :] for ref in kv_refs], 0)
+    key, value = kv_ref[0:SPAN, :], kv_ref[2 * SPAN : 3 * SPAN, :]
     probs, dscores = sub_block(key, value, query_ref, grad_ref, high, of_rows(log_ref, high), of_rows(dot_ref, high))
     scores_ref[...] = dscores
     return dot(dscores, stacked(query_ref, high), (1, 0)), dot(probs, stacked(grad_ref, high), (1, 0))
@@ -182,30 +150,11 @@
     )
 
 
-def outer_kernel(plan_ref, query_ref, grad_ref, kv_ref, log_ref, dot_ref, part_ref, low_ref, half_ref):
-    key_low, value_low = remote_low(query_ref, grad_ref, (kv_ref,), log_ref, dot_ref, low_ref)
+def remote_kernel(j, plan_ref, query_ref, grad_ref, kv_ref, log_ref, dot_ref, _before, part_ref, low_ref, half_ref):
+    key_low, value_low = remote_low(query_ref, grad_ref, kv_ref, log_ref, dot_ref, low_ref)
     part_ref[...] = remote_half(
-        plan_ref[0], query_ref, grad_ref, kv_ref, log_ref, dot_ref, half_ref, key_low, value_low
+        plan_ref[j], query_ref, grad_ref, kv_ref, log_ref, dot_ref, half_ref, key_low, value_low
     ).astype(BF16)
-
-
-def inner_kernel(
-    plan_ref, query_ref, grad_ref, kv1_ref, kv2_ref, log_ref, dot_ref, part1_ref, part2_ref, low_ref, half_ref
-):
-    key_low, value_low = remote_low(query_ref, grad_ref, (kv1_ref, kv2_ref), log_ref, dot_ref, low_ref)
-    for j, (kv_ref, part_ref) in enumerate(((kv1_ref, part1_ref), (kv2_ref, part2_ref))):
-        rows = slice(j * SPAN, (j + 1) * SPAN)
-        part_ref[...] = remote_half(
-            plan_ref[1 + j],
-            query_ref,
-            grad_ref,
-            kv_ref,
-            log_ref,
-            dot_ref,
-            half_ref.at[rows],
-            key_low[rows],
-            value_low[rows],
-        ).astype(BF16)
 
 
 def last_kernel(
@@ -220,8 +169,10 @@
     kv3_ref,
     low1_ref,
     half1_ref,
-    low23_ref,
-    half23_ref,
+    low2_ref,
+    half2_ref,
+    low3_ref,
+    half3_ref,
     _own_scores,
     _key_grad,
     _value_grad,
@@ -240,8 +191,8 @@
     zero = jnp.zeros((SPAN, HD), BF16)
     remotes = (
         (kv1_ref, low1_ref, half1_ref),
-        (kv2_ref, low23_ref.at[low], half23_ref.at[low]),
-        (kv3_ref, low23_ref.at[high], half23_ref.at[high]),
+        (kv2_ref, low2_ref, half2_ref),
+        (kv3_ref, low3_ref, half3_ref),
     )
 
     def query_part(n, rows, keys, scores):
@@ -288,9 +239,9 @@
 def per_device(queries, key_rows, value_rows, out_grad, outputs, log_sum, span_table):
     rows = 2 * SPAN
     place = lax.axis_index(("outer", "inner")).reshape(1)
-    table, key_rows, value_rows, queries, out_grad, outputs, log_sum = (
+    table, key_rows, value_rows = (
         pltpu.with_memory_space_constraint(x, pltpu.HBM)
-        for x in (span_table.T, key_rows, value_rows, queries, out_grad, outputs, log_sum)
+        for x in (span_table.T, key_rows, value_rows)
     )
     packed, plan = pl.pallas_call(
         pack_kernel,
@@ -299,6 +250,7 @@
         out_specs=(VMEM, SMEM),
         scratch_shapes=[pltpu.SMEM((2, OUTER * INNER), jnp.int32), pltpu.SemaphoreType.DMA((3,))],
         compiler_params=PARAMS,
+        cost_estimate=pl.CostEstimate(flops=10**10, bytes_accessed=0, transcendentals=0),
         name="pack",
     )(place, table, key_rows, value_rows)
     arrived = [shifted(packed, a, b) for a, b in STEPS]
@@ -310,43 +262,36 @@
     def spans(count):
         return pltpu.VMEM((count * SPAN, WIDE), BF16)
 
-    queries, out_grad, log_two, row_dot, own_scores, key_own, value_own = pl.pallas_call(
+    log_two, row_dot, own_scores, key_own, value_own = pl.pallas_call(
         load_kernel,
-        out_shape=(wide, wide, small, small, spans(3), total, total),
-        in_specs=[SMEM] + [ANY] * 4 + [VMEM],
-        out_specs=(VMEM,) * 7,
-        scratch_shapes=[wide, small, pltpu.SemaphoreType.DMA((7,))],
+        out_shape=(small, small, spans(3), total, total),
+        in_specs=[SMEM] + [VMEM] * 5,
+        out_specs=(VMEM,) * 5,
         compiler_params=PARAMS,
         cost_estimate=units(2),
         name="load",
     )(plan, queries, out_grad, outputs, log_sum, packed)
-    part1, low1, half1 = pl.pallas_call(
-        outer_kernel,
-        out_shape=(part, spans(1), spans(1)),
-        in_specs=[SMEM] + [VMEM] * 5,
-        out_specs=(VMEM,) * 3,
-        compiler_params=PARAMS,
-        cost_estimate=units(2),
-        name="outer_block",
-    )(plan, queries, out_grad, arrived[0], log_two, row_dot)
-    back = [shifted(part1, -1, 0)]
-    part2, part3, low23, half23 = pl.pallas_call(
-        inner_kernel,
-        out_shape=(part, part, spans(2), spans(2)),
-        in_specs=[SMEM] + [VMEM] * 6,
-        out_specs=(VMEM,) * 4,
-        compiler_params=PARAMS,
-        cost_estimate=units(4),
-        name="inner_blocks",
-    )(plan, queries, out_grad, arrived[1], arrived[2], log_two, row_dot)
-    back += [shifted(part2, -1, -1), shifted(part3, 0, -1)]
+    back, scores = [], []
+    half = row_dot
+    for j, (a, b) in enumerate(STEPS):
+        one, low, half = pl.pallas_call(
+            functools.partial(remote_kernel, j),
+            out_shape=(part, spans(1), spans(1)),
+            in_specs=[SMEM] + [VMEM] * 5 + [ANY],
+            out_specs=(VMEM,) * 3,
+            compiler_params=PARAMS,
+            cost_estimate=units(2),
+            name="remote_block",
+        )(plan, queries, out_grad, arrived[j], log_two, row_dot, half)
+        back.append(shifted(one, -a, -b))
+        scores += [low, half]
     query_grad, _, key_total, value_total = pl.pallas_call(
         last_kernel,
         out_shape=(pltpu.HBM((rows, WIDE), BF16), spans(3), total, total),
-        in_specs=[SMEM] + [VMEM] * 15,
+        in_specs=[SMEM] + [VMEM] * 17,
         out_specs=(ANY, VMEM, VMEM, VMEM),
         scratch_shapes=[wide, pltpu.SemaphoreType.DMA((2,))],
-        input_output_aliases={13: 1, 14: 2, 15: 3},
+        input_output_aliases={15: 1, 16: 2, 17: 3},
         compiler_params=PARAMS,
         cost_estimate=units(4),
         name="last",
@@ -358,10 +303,7 @@
         log_two,
         row_dot,
         *arrived,
-        low1,
-        half1,
-        low23,
-        half23,
+        *scores,
         own_scores,
         key_own,
         value_own,

time: 39.5 us -> 38.4 us (0.972)
  Pallas kernels: 10.7 us -> 9.59 us
  waiting for transfers between devices: 0.89 us -> 0.02 us
  starting transfers between devices: 26 us -> 26.5 us
    pallas_call x3 -> x4, Pallas kernels: 7.85 us -> 6.63 us  [the longest x3 3.97 us: per_device(): pl.pallas_call(functools.partial(remote_kernel, j), out_shape=(part, span...]
    ppermute x6, waiting for transfers between devices: 0.89 us -> 0.02 us  [shifted(): return lax.ppermute(shard, ('outer', 'inner'), pairs)]
    ppermute x6, starting transfers between devices: 26 us -> 26.5 us  [shifted(): return lax.ppermute(shard, ('outer', 'inner'), pairs)]
  transfers between devices with their start and end apart: 6 -> 6, of which waited for: 1 -> 0; matrix products, arithmetic and copies ran while one was open for 0% -> 0% of each run, Pallas kernels for 25% -> 23%
where the time goes in v4:
time: 38.4 us; the launch traced here: 37.7 us
  starting transfers between devices  26.5 us (69%)
  Pallas kernels  9.59 us (25%)
  between operations  0.83 us (2%)
  other arithmetic  0.76 us (2%)
    ppermute x6, starting transfers between devices, shifted(): return lax.ppermute(shard, ('outer', 'inner'), pairs)  26.5 us
    pallas_call x3, Pallas kernels, per_device(): pl.pallas_call(functools.partial(remote_kernel, j), out_shape=(part, span...  3.97 us
    pallas_call x1, Pallas kernels, per_device(): pl.pallas_call(load_kernel, out_shape=(small, small, spans(3), total, tot...  2.66 us
    pallas_call x1, Pallas kernels, per_device(): pl.pallas_call(last_kernel, out_shape=(pltpu.HBM((rows, WIDE), BF16), spa...  1.92 us
    pallas_call x1, Pallas kernels, per_device(): pl.pallas_call(pack_kernel, out_shape=(pltpu.VMEM((2 * rows, HD), BF16),...  1.05 us
  transfers between devices with their start and end apart: 6, of which 0 were waited for; matrix products, arithmetic and copies ran while one was open for 0% of the time, Pallas kernels for 23%

profile of v4, /device:TPU:1, one launch (start us, length us, event | category | flops | bytes accessed | tf_op | source)
XLA Modules:
  0.0 37.7 jit_solution(8070244069374064910)
XLA Ops:
  0.6 0.0 copy-start
  0.6 0.0 copy-start.1
  0.7 0.0 copy-start.2
  0.7 0.0 copy-start.3
  0.7 1.0 %pack.1 = (bf16[512,128]{1,0:T(8,128)(2,1)S(1)}, s32[4]{0:T(128)S(4)}) custom-call(s32[1]{0:T(128)} %bitcast.place_ref, s32[2,512]{1,0:T(2,128)} %bitcast.2, bf16[256,128]{1,0:T(8,128)(2,1)} %key_hbm.1, bf16[256,128]{1,0:T(8,128)(2,1)} %value_hbm.1), custom_call_target="tpu_custom_call" | custom-call | flops 10000000000 | tf_op jit(solution)/shard_map/pack/pallas_call | solution.py:246
  1.7 3.9 %collective-permute-start = (bf16[512,128]{1,0:T(8,128)(2,1)S(1)}, bf16[512,128]{1,0:T(8,128)(2,1)S(1)}, u32[]{:S(2)}, u32[]{:S(2)}) collective-permute-start(bf16[512,128]{1,0:T(8,128)(2,1)S(1)} %get-tuple-element.23.kv_ref), channel_id=1, source_target_pairs={{0,32},{1,33},{2,34},{3,35},{4,36},{5,37},{6,38},{7,39},{8,40},{9,... | collective-permute-start | bytes 393224 | tf_op jit(solution)/shard_map/ppermute | solution.py:236
  5.7 5.2 %collective-permute-start.1 = (bf16[512,128]{1,0:T(8,128)(2,1)S(1)}, bf16[512,128]{1,0:T(8,128)(2,1)S(1)}, u32[]{:S(2)}, u32[]{:S(2)}) collective-permute-start(bf16[512,128]{1,0:T(8,128)(2,1)S(1)} %get-tuple-element.23.kv_ref), channel_id=1, source_target_pairs={{0,1},{1,2},{2,3},{3,4},{4,5},{5,6},{6,7},{7,8},{8,9},{9,10},{10,1... | collective-permute-start | bytes 393224 | tf_op jit(solution)/shard_map/ppermute | solution.py:236
  10.9 2.3 %collective-permute-start.2 = (bf16[512,128]{1,0:T(8,128)(2,1)S(1)}, bf16[512,128]{1,0:T(8,128)(2,1)S(1)}, u32[]{:S(2)}, u32[]{:S(2)}) collective-permute-start(bf16[512,128]{1,0:T(8,128)(2,1)S(1)} %get-tuple-element.23.kv_ref), channel_id=1, source_target_pairs={{0,33},{1,34},{2,35},{3,36},{4,37},{5,38},{6,39},{7,40},{8,41},{9,... | collective-permute-start | bytes 393224 | tf_op jit(solution)/shard_map/ppermute | solution.py:236
  13.2 0.0 copy-done
  13.2 0.0 copy-done.1
  13.2 0.0 copy-done.2
  13.2 0.0 copy-done.3
  13.2 2.7 %load.1 = (f32[16,256]{1,0:T(8,128)S(1)}, f32[16,256]{1,0:T(8,128)S(1)}, bf16[384,2048]{1,0:T(8,128)(2,1)S(1)}, f32[256,128]{1,0:T(8,128)S(1)}, f32[256,128]{1,0:T(8,128)S(1)}) custom-call(s32[4]{0:T(128)S(4)} %get-tuple-element.22.plan_ref, bf16[256,2048]{1,0:T(8,128)(2,1)S(1)} %copy-done, bf16[256,2048]{1,0:T(8,128)(2,1)S(1)} %copy-done.1, ...), custom_call_target="tpu_custom_call" | custom-call | flops 671088640 | bytes 1048576 | tf_op jit(solution)/shard_map/load/pallas_call | solution.py:265
  15.9 0.0 collective-permute-done.kv_ref.kv1_ref
  15.9 1.3 %remote_block.3 = (bf16[512,128]{1,0:T(8,128)(2,1)S(1)}, bf16[128,2048]{1,0:T(8,128)(2,1)S(1)}, bf16[128,2048]{1,0:T(8,128)(2,1)S(1)}) custom-call(s32[4]{0:T(128)S(4)} %get-tuple-element.22.plan_ref, bf16[256,2048]{1,0:T(8,128)(2,1)S(1)} %copy-done, bf16[256,2048]{1,0:T(8,128)(2,1)S(1)} %copy-done.1, ...), custom_call_target="tpu_custom_call" | custom-call | flops 671088640 | bytes 1048576 | tf_op jit(solution)/shard_map/remote_block/pallas_call | solution.py:277
  17.2 3.6 %collective-permute-start.3 = (bf16[512,128]{1,0:T(8,128)(2,1)S(1)}, bf16[512,128]{1,0:T(8,128)(2,1)S(1)}, u32[]{:S(2)}, u32[]{:S(2)}) collective-permute-start(bf16[512,128]{1,0:T(8,128)(2,1)S(1)} %get-tuple-element.37), channel_id=1, source_target_pairs={{0,480},{1,481},{2,482},{3,483},{4,484},{5,485},{6,486},{7,487},{8... | collective-permute-start | bytes 393224 | tf_op jit(solution)/shard_map/ppermute | solution.py:236
  20.8 0.0 collective-permute-done.1.kv_ref.kv2_ref
  20.9 1.3 %remote_block.4 = (bf16[512,128]{1,0:T(8,128)(2,1)S(1)}, bf16[128,2048]{1,0:T(8,128)(2,1)S(1)}, bf16[128,2048]{1,0:T(8,128)(2,1)S(1)}) custom-call(s32[4]{0:T(128)S(4)} %get-tuple-element.22.plan_ref, bf16[256,2048]{1,0:T(8,128)(2,1)S(1)} %copy-done, bf16[256,2048]{1,0:T(8,128)(2,1)S(1)} %copy-done.1, ...), custom_call_target="tpu_custom_call" | custom-call | flops 671088640 | bytes 1048576 | tf_op jit(solution)/shard_map/remote_block/pallas_call | solution.py:277
  22.2 5.6 %collective-permute-start.4 = (bf16[512,128]{1,0:T(8,128)(2,1)S(1)}, bf16[512,128]{1,0:T(8,128)(2,1)S(1)}, u32[]{:S(2)}, u32[]{:S(2)}) collective-permute-start(bf16[512,128]{1,0:T(8,128)(2,1)S(1)} %get-tuple-element.38), channel_id=1, source_target_pairs={{0,31},{1,0},{2,1},{3,2},{4,3},{5,4},{6,5},{7,6},{8,7},{9,8},{10,9... | collective-permute-start | bytes 393224 | tf_op jit(solution)/shard_map/ppermute | solution.py:236
  27.7 0.0 collective-permute-done.2.kv_ref.kv3_ref
  27.7 1.3 %remote_block.5 = (bf16[512,128]{1,0:T(8,128)(2,1)S(1)}, bf16[128,2048]{1,0:T(8,128)(2,1)S(1)}, bf16[128,2048]{1,0:T(8,128)(2,1)S(1)}) custom-call(s32[4]{0:T(128)S(4)} %get-tuple-element.22.plan_ref, bf16[256,2048]{1,0:T(8,128)(2,1)S(1)} %copy-done, bf16[256,2048]{1,0:T(8,128)(2,1)S(1)} %copy-done.1, ...), custom_call_target="tpu_custom_call" | custom-call | flops 671088640 | bytes 1048576 | tf_op jit(solution)/shard_map/remote_block/pallas_call | solution.py:277
  29.1 5.9 %collective-permute-start.5 = (bf16[512,128]{1,0:T(8,128)(2,1)S(1)}, bf16[512,128]{1,0:T(8,128)(2,1)S(1)}, u32[]{:S(2)}, u32[]{:S(2)}) collective-permute-start(bf16[512,128]{1,0:T(8,128)(2,1)S(1)} %get-tuple-element.39), channel_id=1, source_target_pairs={{0,511},{1,480},{2,481},{3,482},{4,483},{5,484},{6,485},{7,486},{8... | collective-permute-start | bytes 393224 | tf_op jit(solution)/shard_map/ppermute | solution.py:236
  35.0 1.9 %last.1 = (bf16[256,2048]{1,0:T(8,128)(2,1)}, bf16[384,2048]{1,0:T(8,128)(2,1)S(1)}, f32[256,128]{1,0:T(8,128)S(1)}, f32[256,128]{1,0:T(8,128)S(1)}) custom-call(s32[4]{0:T(128)S(4)} %get-tuple-element.22.plan_ref, bf16[256,2048]{1,0:T(8,128)(2,1)S(1)} %copy-done, ...), custom_call_target="tpu_custom_call", output_to_operand_aliasing={{1}: (15, {}), {2}: (16, {}), {3}: (17, {})} | custom-call | flops 1342177280 | bytes 1048576 | tf_op jit(solution)/shard_map/last/pallas_call | solution.py:288
  36.9 0.0 collective-permute-done.3
  36.9 0.0 collective-permute-done.4
  36.9 0.0 collective-permute-done.5
  36.9 0.8 %convert_add_fusion = (f32[256,128]{1,0:T(8,128)}, f32[256,128]{1,0:T(8,128)}) fusion(f32[256,128]{1,0:T(8,128)S(1)} %get-tuple-element.40, bf16[512,128]{1,0:T(8,128)(2,1)S(1)} %collective-permute-done.5, bf16[512,128]{1,0:T(8,128)(2,1)S(1)} %collective-permute-done.4, bf16[512,128]{1,0:T(8,128)(2,1)S(1)} %collective-permute-done.3, ...), kind=kLoop, calls=%fused_computation | loop fusion | flops 425984 | bytes 917504 | tf_op jit(solution)/shard_map/add | solution.py:313
Async XLA Ops:
  0.6 12.6 %copy-start = (bf16[256,2048]{1,0:T(8,128)(2,1)S(1)}, bf16[256,2048]{1,0:T(8,128)(2,1)}, u32[]{:S(2)}) copy-start(bf16[256,2048]{1,0:T(8,128)(2,1)} %query_ref.9) | copy-start | bytes 3145732
  0.6 12.6 %copy-start.1 = (bf16[256,2048]{1,0:T(8,128)(2,1)S(1)}, bf16[256,2048]{1,0:T(8,128)(2,1)}, u32[]{:S(2)}) copy-start(bf16[256,2048]{1,0:T(8,128)(2,1)} %grad_ref.9) | copy-start | bytes 3145732
  0.7 12.6 %copy-start.2 = (bf16[256,2048]{1,0:T(8,128)(2,1)S(1)}, bf16[256,2048]{1,0:T(8,128)(2,1)}, u32[]{:S(2)}) copy-start(bf16[256,2048]{1,0:T(8,128)(2,1)} %out_ref.1) | copy-start | bytes 3145732
  0.7 12.6 %copy-start.3 = (f32[16,256]{1,0:T(8,128)S(1)}, f32[16,256]{1,0:T(8,128)}, u32[]{:S(2)}) copy-start(f32[16,256]{1,0:T(8,128)} %sum_ref.1) | copy-start | bytes 49156
  1.7 14.2 %collective-permute-start = (bf16[512,128]{1,0:T(8,128)(2,1)S(1)}, bf16[512,128]{1,0:T(8,128)(2,1)S(1)}, u32[]{:S(2)}, u32[]{:S(2)}) collective-permute-start(bf16[512,128]{1,0:T(8,128)(2,1)S(1)} %get-tuple-element.23.kv_ref), channel_id=1, source_target_pairs={{0,32},{1,33},{2,34},{3,35},{4,36},{5,37},{6,38},{7,39},{8,40},{9,... | collective-permute-start | bytes 393224 | tf_op jit(solution)/shard_map/ppermute | solution.py:236
  5.7 15.2 %collective-permute-start.1 = (bf16[512,128]{1,0:T(8,128)(2,1)S(1)}, bf16[512,128]{1,0:T(8,128)(2,1)S(1)}, u32[]{:S(2)}, u32[]{:S(2)}) collective-permute-start(bf16[512,128]{1,0:T(8,128)(2,1)S(1)} %get-tuple-element.23.kv_ref), channel_id=1, source_target_pairs={{0,1},{1,2},{2,3},{3,4},{4,5},{5,6},{6,7},{7,8},{8,9},{9,10},{10,1... | collective-permute-start | bytes 393224 | tf_op jit(solution)/shard_map/ppermute | solution.py:236
  10.9 16.8 %collective-permute-start.2 = (bf16[512,128]{1,0:T(8,128)(2,1)S(1)}, bf16[512,128]{1,0:T(8,128)(2,1)S(1)}, u32[]{:S(2)}, u32[]{:S(2)}) collective-permute-start(bf16[512,128]{1,0:T(8,128)(2,1)S(1)} %get-tuple-element.23.kv_ref), channel_id=1, source_target_pairs={{0,33},{1,34},{2,35},{3,36},{4,37},{5,38},{6,39},{7,40},{8,41},{9,... | collective-permute-start | bytes 393224 | tf_op jit(solution)/shard_map/ppermute | solution.py:236
  17.2 19.7 %collective-permute-start.3 = (bf16[512,128]{1,0:T(8,128)(2,1)S(1)}, bf16[512,128]{1,0:T(8,128)(2,1)S(1)}, u32[]{:S(2)}, u32[]{:S(2)}) collective-permute-start(bf16[512,128]{1,0:T(8,128)(2,1)S(1)} %get-tuple-element.37), channel_id=1, source_target_pairs={{0,480},{1,481},{2,482},{3,483},{4,484},{5,485},{6,486},{7,487},{8... | collective-permute-start | bytes 393224 | tf_op jit(solution)/shard_map/ppermute | solution.py:236
  22.2 14.8 %collective-permute-start.4 = (bf16[512,128]{1,0:T(8,128)(2,1)S(1)}, bf16[512,128]{1,0:T(8,128)(2,1)S(1)}, u32[]{:S(2)}, u32[]{:S(2)}) collective-permute-start(bf16[512,128]{1,0:T(8,128)(2,1)S(1)} %get-tuple-element.38), channel_id=1, source_target_pairs={{0,31},{1,0},{2,1},{3,2},{4,3},{5,4},{6,5},{7,6},{8,7},{9,8},{10,9... | collective-permute-start | bytes 393224 | tf_op jit(solution)/shard_map/ppermute | solution.py:236
  29.1 7.9 %collective-permute-start.5 = (bf16[512,128]{1,0:T(8,128)(2,1)S(1)}, bf16[512,128]{1,0:T(8,128)(2,1)S(1)}, u32[]{:S(2)}, u32[]{:S(2)}) collective-permute-start(bf16[512,128]{1,0:T(8,128)(2,1)S(1)} %get-tuple-element.39), channel_id=1, source_target_pairs={{0,511},{1,480},{2,481},{3,482},{4,483},{5,484},{6,485},{7,486},{8... | collective-permute-start | bytes 393224 | tf_op jit(solution)/shard_map/ppermute | solution.py:236

commit v5 on v4

--- a/solution.py
+++ b/solution.py
@@ -64,8 +64,8 @@
         pltpu.make_async_copy(key_hbm, packed_ref.at[0:rows], sems.at[1]),
         pltpu.make_async_copy(value_hbm, packed_ref.at[rows : 2 * rows], sems.at[2]),
     ]
-    for copy in copies:
-        copy.start()
+    for n in (1, 2, 0):
+        copies[n].start()
     outer, inner = place_ref[0] // INNER, place_ref[0] % INNER
     plan_ref[len(STEPS)] = (inner < EARLY).astype(jnp.int32)
     copies[0].wait()
@@ -216,6 +216,23 @@
     copy_low = query_part(0, low, keys, scores)
     copy_high.wait()
     copy_low.wait()
+
+
+def total_kernel(key_ref, value_ref, one_ref, two_ref, three_ref, key_hbm, value_hbm, key_sum_ref, value_sum_ref, sems):
+    rows = 2 * SPAN
+    copies = []
+    for n, (own, target, out, factor) in enumerate(
+        ((key_ref, key_sum_ref, key_hbm, FACTOR), (value_ref, value_sum_ref, value_hbm, None))
+    ):
+        part = slice(n * rows, (n + 1) * rows)
+        total = own[...]
+        for ref in (one_ref, two_ref, three_ref):
+            total = total + ref[part, :].astype(F32)
+        target[...] = total if factor is None else total * factor
+        copies.append(pltpu.make_async_copy(target, out, sems.at[n]))
+        copies[n].start()
+    for copy in copies:
+        copy.wait()
 
 
 VMEM = pl.BlockSpec(memory_space=pltpu.VMEM)
@@ -308,10 +325,16 @@
         key_own,
         value_own,
     )
-    for one in back:
-        key_total = key_total + one[:rows].astype(F32)
-        value_total = value_total + one[rows:].astype(F32)
-    return (query_grad, key_total * FACTOR, value_total)
+    key_total, value_total = pl.pallas_call(
+        total_kernel,
+        out_shape=(pltpu.HBM((rows, HD), F32), pltpu.HBM((rows, HD), F32)),
+        in_specs=[VMEM] * 5,
+        out_specs=(ANY, ANY),
+        scratch_shapes=[total, total, pltpu.SemaphoreType.DMA((2,))],
+        compiler_params=PARAMS,
+        name="totals",
+    )(key_total, value_total, *back)
+    return (query_grad, key_total, value_total)
 
 
 def solution(mesh):

time: 38.4 us -> 38.4 us (level)
  Pallas kernels: 9.59 us -> 10.4 us
  other arithmetic: 0.76 us -> 0 us
    add x1 -> x0, other arithmetic: 0.76 us -> none  [per_device(): value_total = value_total + one[rows:].astype(F32)]
    pallas_call x0 -> x1, Pallas kernels: none -> 0.75 us  [per_device(): pl.pallas_call(total_kernel, out_shape=(pltpu.HBM((rows, HD), F32), pltpu...]
where the time goes in v5:
time: 38.4 us; the launch traced here: 37.7 us
  starting transfers between devices  26.5 us (69%)
  Pallas kernels  10.4 us (27%)
  between operations  0.83 us (2%)
    ppermute x6, starting transfers between devices, shifted(): return lax.ppermute(shard, ('outer', 'inner'), pairs)  26.5 us
    pallas_call x3, Pallas kernels, per_device(): pl.pallas_call(functools.partial(remote_kernel, j), out_shape=(part, span...  3.97 us
    pallas_call x1, Pallas kernels, per_device(): pl.pallas_call(load_kernel, out_shape=(small, small, spans(3), total, tot...  2.66 us
    pallas_call x1, Pallas kernels, per_device(): pl.pallas_call(last_kernel, out_shape=(pltpu.HBM((rows, WIDE), BF16), spa...  1.92 us
    pallas_call x1, Pallas kernels, per_device(): pl.pallas_call(pack_kernel, out_shape=(pltpu.VMEM((2 * rows, HD), BF16),...  1.05 us
  transfers between devices with their start and end apart: 6, of which 0 were waited for; matrix products, arithmetic and copies ran while one was open for 0% of the time, Pallas kernels for 23%

profile of v5, /device:TPU:1, one launch (start us, length us, event | category | flops | bytes accessed | tf_op | source)
XLA Modules:
  0.0 37.7 jit_solution(2074449103401604036)
XLA Ops:
  0.6 0.0 copy-start
  0.6 0.0 copy-start.1
  0.7 0.0 copy-start.2
  0.7 0.0 copy-start.3
  0.7 1.0 %pack.1 = (bf16[512,128]{1,0:T(8,128)(2,1)S(1)}, s32[4]{0:T(128)S(4)}) custom-call(s32[1]{0:T(128)} %bitcast.place_ref, s32[2,512]{1,0:T(2,128)} %bitcast.2, bf16[256,128]{1,0:T(8,128)(2,1)} %key_hbm.1, bf16[256,128]{1,0:T(8,128)(2,1)} %value_hbm.1), custom_call_target="tpu_custom_call" | custom-call | flops 10000000000 | tf_op jit(solution)/shard_map/pack/pallas_call | solution.py:263
  1.7 3.9 %collective-permute-start = (bf16[512,128]{1,0:T(8,128)(2,1)S(1)}, bf16[512,128]{1,0:T(8,128)(2,1)S(1)}, u32[]{:S(2)}, u32[]{:S(2)}) collective-permute-start(bf16[512,128]{1,0:T(8,128)(2,1)S(1)} %get-tuple-element.25.kv_ref), channel_id=1, source_target_pairs={{0,32},{1,33},{2,34},{3,35},{4,36},{5,37},{6,38},{7,39},{8,40},{9,... | collective-permute-start | bytes 393224 | tf_op jit(solution)/shard_map/ppermute | solution.py:253
  5.7 5.2 %collective-permute-start.1 = (bf16[512,128]{1,0:T(8,128)(2,1)S(1)}, bf16[512,128]{1,0:T(8,128)(2,1)S(1)}, u32[]{:S(2)}, u32[]{:S(2)}) collective-permute-start(bf16[512,128]{1,0:T(8,128)(2,1)S(1)} %get-tuple-element.25.kv_ref), channel_id=1, source_target_pairs={{0,1},{1,2},{2,3},{3,4},{4,5},{5,6},{6,7},{7,8},{8,9},{9,10},{10,1... | collective-permute-start | bytes 393224 | tf_op jit(solution)/shard_map/ppermute | solution.py:253
  10.9 2.3 %collective-permute-start.2 = (bf16[512,128]{1,0:T(8,128)(2,1)S(1)}, bf16[512,128]{1,0:T(8,128)(2,1)S(1)}, u32[]{:S(2)}, u32[]{:S(2)}) collective-permute-start(bf16[512,128]{1,0:T(8,128)(2,1)S(1)} %get-tuple-element.25.kv_ref), channel_id=1, source_target_pairs={{0,33},{1,34},{2,35},{3,36},{4,37},{5,38},{6,39},{7,40},{8,41},{9,... | collective-permute-start | bytes 393224 | tf_op jit(solution)/shard_map/ppermute | solution.py:253
  13.2 0.0 copy-done
  13.2 0.0 copy-done.1
  13.2 0.0 copy-done.2
  13.2 0.0 copy-done.3
  13.2 2.7 %load.1 = (f32[16,256]{1,0:T(8,128)S(1)}, f32[16,256]{1,0:T(8,128)S(1)}, bf16[384,2048]{1,0:T(8,128)(2,1)S(1)}, f32[256,128]{1,0:T(8,128)S(1)}, f32[256,128]{1,0:T(8,128)S(1)}) custom-call(s32[4]{0:T(128)S(4)} %get-tuple-element.24.plan_ref, bf16[256,2048]{1,0:T(8,128)(2,1)S(1)} %copy-done, bf16[256,2048]{1,0:T(8,128)(2,1)S(1)} %copy-done.1, ...), custom_call_target="tpu_custom_call" | custom-call | flops 671088640 | bytes 1048576 | tf_op jit(solution)/shard_map/load/pallas_call | solution.py:282
  15.9 0.0 collective-permute-done.kv_ref.kv1_ref
  15.9 1.3 %remote_block.3 = (bf16[512,128]{1,0:T(8,128)(2,1)S(1)}, bf16[128,2048]{1,0:T(8,128)(2,1)S(1)}, bf16[128,2048]{1,0:T(8,128)(2,1)S(1)}) custom-call(s32[4]{0:T(128)S(4)} %get-tuple-element.24.plan_ref, bf16[256,2048]{1,0:T(8,128)(2,1)S(1)} %copy-done, bf16[256,2048]{1,0:T(8,128)(2,1)S(1)} %copy-done.1, ...), custom_call_target="tpu_custom_call" | custom-call | flops 671088640 | bytes 1048576 | tf_op jit(solution)/shard_map/remote_block/pallas_call | solution.py:294
  17.3 3.6 %collective-permute-start.3 = (bf16[512,128]{1,0:T(8,128)(2,1)S(1)}, bf16[512,128]{1,0:T(8,128)(2,1)S(1)}, u32[]{:S(2)}, u32[]{:S(2)}) collective-permute-start(bf16[512,128]{1,0:T(8,128)(2,1)S(1)} %get-tuple-element.40), channel_id=1, source_target_pairs={{0,480},{1,481},{2,482},{3,483},{4,484},{5,485},{6,486},{7,487},{8... | collective-permute-start | bytes 393224 | tf_op jit(solution)/shard_map/ppermute | solution.py:253
  20.8 0.0 collective-permute-done.1.kv_ref.kv2_ref
  20.8 1.3 %remote_block.4 = (bf16[512,128]{1,0:T(8,128)(2,1)S(1)}, bf16[128,2048]{1,0:T(8,128)(2,1)S(1)}, bf16[128,2048]{1,0:T(8,128)(2,1)S(1)}) custom-call(s32[4]{0:T(128)S(4)} %get-tuple-element.24.plan_ref, bf16[256,2048]{1,0:T(8,128)(2,1)S(1)} %copy-done, bf16[256,2048]{1,0:T(8,128)(2,1)S(1)} %copy-done.1, ...), custom_call_target="tpu_custom_call" | custom-call | flops 671088640 | bytes 1048576 | tf_op jit(solution)/shard_map/remote_block/pallas_call | solution.py:294
  22.2 5.6 %collective-permute-start.4 = (bf16[512,128]{1,0:T(8,128)(2,1)S(1)}, bf16[512,128]{1,0:T(8,128)(2,1)S(1)}, u32[]{:S(2)}, u32[]{:S(2)}) collective-permute-start(bf16[512,128]{1,0:T(8,128)(2,1)S(1)} %get-tuple-element.41), channel_id=1, source_target_pairs={{0,31},{1,0},{2,1},{3,2},{4,3},{5,4},{6,5},{7,6},{8,7},{9,8},{10,9... | collective-permute-start | bytes 393224 | tf_op jit(solution)/shard_map/ppermute | solution.py:253
  27.7 0.0 collective-permute-done.2.kv_ref.kv3_ref
  27.7 1.3 %remote_block.5 = (bf16[512,128]{1,0:T(8,128)(2,1)S(1)}, bf16[128,2048]{1,0:T(8,128)(2,1)S(1)}, bf16[128,2048]{1,0:T(8,128)(2,1)S(1)}) custom-call(s32[4]{0:T(128)S(4)} %get-tuple-element.24.plan_ref, bf16[256,2048]{1,0:T(8,128)(2,1)S(1)} %copy-done, bf16[256,2048]{1,0:T(8,128)(2,1)S(1)} %copy-done.1, ...), custom_call_target="tpu_custom_call" | custom-call | flops 671088640 | bytes 1048576 | tf_op jit(solution)/shard_map/remote_block/pallas_call | solution.py:294
  29.1 5.9 %collective-permute-start.5 = (bf16[512,128]{1,0:T(8,128)(2,1)S(1)}, bf16[512,128]{1,0:T(8,128)(2,1)S(1)}, u32[]{:S(2)}, u32[]{:S(2)}) collective-permute-start(bf16[512,128]{1,0:T(8,128)(2,1)S(1)} %get-tuple-element.42), channel_id=1, source_target_pairs={{0,511},{1,480},{2,481},{3,482},{4,483},{5,484},{6,485},{7,486},{8... | collective-permute-start | bytes 393224 | tf_op jit(solution)/shard_map/ppermute | solution.py:253
  35.0 1.9 %last.1 = (bf16[256,2048]{1,0:T(8,128)(2,1)}, bf16[384,2048]{1,0:T(8,128)(2,1)S(1)}, f32[256,128]{1,0:T(8,128)S(1)}, f32[256,128]{1,0:T(8,128)S(1)}) custom-call(s32[4]{0:T(128)S(4)} %get-tuple-element.24.plan_ref, bf16[256,2048]{1,0:T(8,128)(2,1)S(1)} %copy-done, ...), custom_call_target="tpu_custom_call", output_to_operand_aliasing={{1}: (15, {}), {2}: (16, {}), {3}: (17, {})} | custom-call | flops 1342177280 | bytes 1048576 | tf_op jit(solution)/shard_map/last/pallas_call | solution.py:305
  36.9 0.0 collective-permute-done.3.one_ref
  36.9 0.0 collective-permute-done.4.two_ref
  36.9 0.0 collective-permute-done.5.three_ref
  37.0 0.8 %totals.1 = (f32[256,128]{1,0:T(8,128)}, f32[256,128]{1,0:T(8,128)}) custom-call(f32[256,128]{1,0:T(8,128)S(1)} %get-tuple-element.38.key_ref, f32[256,128]{1,0:T(8,128)S(1)} %get-tuple-element.39.value_ref, bf16[512,128]{1,0:T(8,128)(2,1)S(1)} %collective-permute-done.3.one_ref, bf16[512,128]{1,0:T(8,128)(2,1)S(1)} %collective-permute-done.4.two_ref, ...), custom_call_target="tpu_custom_call" | custom-call | tf_op jit(solution)/shard_map/totals/pallas_call | solution.py:328
Async XLA Ops:
  0.6 12.6 %copy-start = (bf16[256,2048]{1,0:T(8,128)(2,1)S(1)}, bf16[256,2048]{1,0:T(8,128)(2,1)}, u32[]{:S(2)}) copy-start(bf16[256,2048]{1,0:T(8,128)(2,1)} %query_ref.9) | copy-start | bytes 3145732
  0.6 12.6 %copy-start.1 = (bf16[256,2048]{1,0:T(8,128)(2,1)S(1)}, bf16[256,2048]{1,0:T(8,128)(2,1)}, u32[]{:S(2)}) copy-start(bf16[256,2048]{1,0:T(8,128)(2,1)} %grad_ref.9) | copy-start | bytes 3145732
  0.7 12.6 %copy-start.2 = (bf16[256,2048]{1,0:T(8,128)(2,1)S(1)}, bf16[256,2048]{1,0:T(8,128)(2,1)}, u32[]{:S(2)}) copy-start(bf16[256,2048]{1,0:T(8,128)(2,1)} %out_ref.1) | copy-start | bytes 3145732
  0.7 12.6 %copy-start.3 = (f32[16,256]{1,0:T(8,128)S(1)}, f32[16,256]{1,0:T(8,128)}, u32[]{:S(2)}) copy-start(f32[16,256]{1,0:T(8,128)} %sum_ref.1) | copy-start | bytes 49156
  1.7 14.2 %collective-permute-start = (bf16[512,128]{1,0:T(8,128)(2,1)S(1)}, bf16[512,128]{1,0:T(8,128)(2,1)S(1)}, u32[]{:S(2)}, u32[]{:S(2)}) collective-permute-start(bf16[512,128]{1,0:T(8,128)(2,1)S(1)} %get-tuple-element.25.kv_ref), channel_id=1, source_target_pairs={{0,32},{1,33},{2,34},{3,35},{4,36},{5,37},{6,38},{7,39},{8,40},{9,... | collective-permute-start | bytes 393224 | tf_op jit(solution)/shard_map/ppermute | solution.py:253
  5.7 15.1 %collective-permute-start.1 = (bf16[512,128]{1,0:T(8,128)(2,1)S(1)}, bf16[512,128]{1,0:T(8,128)(2,1)S(1)}, u32[]{:S(2)}, u32[]{:S(2)}) collective-permute-start(bf16[512,128]{1,0:T(8,128)(2,1)S(1)} %get-tuple-element.25.kv_ref), channel_id=1, source_target_pairs={{0,1},{1,2},{2,3},{3,4},{4,5},{5,6},{6,7},{7,8},{8,9},{9,10},{10,1... | collective-permute-start | bytes 393224 | tf_op jit(solution)/shard_map/ppermute | solution.py:253
  10.9 16.8 %collective-permute-start.2 = (bf16[512,128]{1,0:T(8,128)(2,1)S(1)}, bf16[512,128]{1,0:T(8,128)(2,1)S(1)}, u32[]{:S(2)}, u32[]{:S(2)}) collective-permute-start(bf16[512,128]{1,0:T(8,128)(2,1)S(1)} %get-tuple-element.25.kv_ref), channel_id=1, source_target_pairs={{0,33},{1,34},{2,35},{3,36},{4,37},{5,38},{6,39},{7,40},{8,41},{9,... | collective-permute-start | bytes 393224 | tf_op jit(solution)/shard_map/ppermute | solution.py:253
  17.3 19.7 %collective-permute-start.3 = (bf16[512,128]{1,0:T(8,128)(2,1)S(1)}, bf16[512,128]{1,0:T(8,128)(2,1)S(1)}, u32[]{:S(2)}, u32[]{:S(2)}) collective-permute-start(bf16[512,128]{1,0:T(8,128)(2,1)S(1)} %get-tuple-element.40), channel_id=1, source_target_pairs={{0,480},{1,481},{2,482},{3,483},{4,484},{5,485},{6,486},{7,487},{8... | collective-permute-start | bytes 393224 | tf_op jit(solution)/shard_map/ppermute | solution.py:253
  22.2 14.8 %collective-permute-start.4 = (bf16[512,128]{1,0:T(8,128)(2,1)S(1)}, bf16[512,128]{1,0:T(8,128)(2,1)S(1)}, u32[]{:S(2)}, u32[]{:S(2)}) collective-permute-start(bf16[512,128]{1,0:T(8,128)(2,1)S(1)} %get-tuple-element.41), channel_id=1, source_target_pairs={{0,31},{1,0},{2,1},{3,2},{4,3},{5,4},{6,5},{7,6},{8,7},{9,8},{10,9... | collective-permute-start | bytes 393224 | tf_op jit(solution)/shard_map/ppermute | solution.py:253
  29.1 7.9 %collective-permute-start.5 = (bf16[512,128]{1,0:T(8,128)(2,1)S(1)}, bf16[512,128]{1,0:T(8,128)(2,1)S(1)}, u32[]{:S(2)}, u32[]{:S(2)}) collective-permute-start(bf16[512,128]{1,0:T(8,128)(2,1)S(1)} %get-tuple-element.42), channel_id=1, source_target_pairs={{0,511},{1,480},{2,481},{3,482},{4,483},{5,484},{6,485},{7,486},{8... | collective-permute-start | bytes 393224 | tf_op jit(solution)/shard_map/ppermute | solution.py:253

commit v6 on v4

--- a/solution.py
+++ b/solution.py
@@ -18,7 +18,7 @@
 OUTER = 16
 INNER = 32
 STEPS = ((1, 0), (0, 1), (1, 1))
-EARLY = 4
+EARLY = 2
 LOG2E = math.log2(math.e)
 
 

time: 38.4 us -> 38.4 us (level)
  no operation moved by 1% of the time
where the time goes in v6:
time: 38.4 us; the launch traced here: 37.7 us
  starting transfers between devices  26.5 us (69%)
  Pallas kernels  9.59 us (25%)
  between operations  0.83 us (2%)
  other arithmetic  0.76 us (2%)
    ppermute x6, starting transfers between devices, shifted(): return lax.ppermute(shard, ('outer', 'inner'), pairs)  26.5 us
    pallas_call x3, Pallas kernels, per_device(): pl.pallas_call(functools.partial(remote_kernel, j), out_shape=(part, span...  3.97 us
    pallas_call x1, Pallas kernels, per_device(): pl.pallas_call(load_kernel, out_shape=(small, small, spans(3), total, tot...  2.66 us
    pallas_call x1, Pallas kernels, per_device(): pl.pallas_call(last_kernel, out_shape=(pltpu.HBM((rows, WIDE), BF16), spa...  1.92 us
    pallas_call x1, Pallas kernels, per_device(): pl.pallas_call(pack_kernel, out_shape=(pltpu.VMEM((2 * rows, HD), BF16),...  1.05 us
  transfers between devices with their start and end apart: 6, of which 0 were waited for; matrix products, arithmetic and copies ran while one was open for 0% of the time, Pallas kernels for 23%

profile of v6, /device:TPU:1, one launch (start us, length us, event | category | flops | bytes accessed | tf_op | source)
XLA Modules:
  0.0 37.7 jit_solution(7335227801436946501)
XLA Ops:
  0.6 0.0 copy-start
  0.6 0.0 copy-start.1
  0.7 0.0 copy-start.2
  0.7 0.0 copy-start.3
  0.7 1.0 %pack.1 = (bf16[512,128]{1,0:T(8,128)(2,1)S(1)}, s32[4]{0:T(128)S(4)}) custom-call(s32[1]{0:T(128)} %bitcast.place_ref, s32[2,512]{1,0:T(2,128)} %bitcast.2, bf16[256,128]{1,0:T(8,128)(2,1)} %key_hbm.1, bf16[256,128]{1,0:T(8,128)(2,1)} %value_hbm.1), custom_call_target="tpu_custom_call" | custom-call | flops 10000000000 | tf_op jit(solution)/shard_map/pack/pallas_call | solution.py:246
  1.7 3.9 %collective-permute-start = (bf16[512,128]{1,0:T(8,128)(2,1)S(1)}, bf16[512,128]{1,0:T(8,128)(2,1)S(1)}, u32[]{:S(2)}, u32[]{:S(2)}) collective-permute-start(bf16[512,128]{1,0:T(8,128)(2,1)S(1)} %get-tuple-element.23.kv_ref), channel_id=1, source_target_pairs={{0,32},{1,33},{2,34},{3,35},{4,36},{5,37},{6,38},{7,39},{8,40},{9,... | collective-permute-start | bytes 393224 | tf_op jit(solution)/shard_map/ppermute | solution.py:236
  5.7 5.2 %collective-permute-start.1 = (bf16[512,128]{1,0:T(8,128)(2,1)S(1)}, bf16[512,128]{1,0:T(8,128)(2,1)S(1)}, u32[]{:S(2)}, u32[]{:S(2)}) collective-permute-start(bf16[512,128]{1,0:T(8,128)(2,1)S(1)} %get-tuple-element.23.kv_ref), channel_id=1, source_target_pairs={{0,1},{1,2},{2,3},{3,4},{4,5},{5,6},{6,7},{7,8},{8,9},{9,10},{10,1... | collective-permute-start | bytes 393224 | tf_op jit(solution)/shard_map/ppermute | solution.py:236
  10.9 2.3 %collective-permute-start.2 = (bf16[512,128]{1,0:T(8,128)(2,1)S(1)}, bf16[512,128]{1,0:T(8,128)(2,1)S(1)}, u32[]{:S(2)}, u32[]{:S(2)}) collective-permute-start(bf16[512,128]{1,0:T(8,128)(2,1)S(1)} %get-tuple-element.23.kv_ref), channel_id=1, source_target_pairs={{0,33},{1,34},{2,35},{3,36},{4,37},{5,38},{6,39},{7,40},{8,41},{9,... | collective-permute-start | bytes 393224 | tf_op jit(solution)/shard_map/ppermute | solution.py:236
  13.2 0.0 copy-done
  13.2 0.0 copy-done.1
  13.2 0.0 copy-done.2
  13.2 0.0 copy-done.3
  13.2 2.7 %load.1 = (f32[16,256]{1,0:T(8,128)S(1)}, f32[16,256]{1,0:T(8,128)S(1)}, bf16[384,2048]{1,0:T(8,128)(2,1)S(1)}, f32[256,128]{1,0:T(8,128)S(1)}, f32[256,128]{1,0:T(8,128)S(1)}) custom-call(s32[4]{0:T(128)S(4)} %get-tuple-element.22.plan_ref, bf16[256,2048]{1,0:T(8,128)(2,1)S(1)} %copy-done, bf16[256,2048]{1,0:T(8,128)(2,1)S(1)} %copy-done.1, ...), custom_call_target="tpu_custom_call" | custom-call | flops 671088640 | bytes 1048576 | tf_op jit(solution)/shard_map/load/pallas_call | solution.py:265
  15.9 0.0 collective-permute-done.kv_ref.kv1_ref
  15.9 1.3 %remote_block.3 = (bf16[512,128]{1,0:T(8,128)(2,1)S(1)}, bf16[128,2048]{1,0:T(8,128)(2,1)S(1)}, bf16[128,2048]{1,0:T(8,128)(2,1)S(1)}) custom-call(s32[4]{0:T(128)S(4)} %get-tuple-element.22.plan_ref, bf16[256,2048]{1,0:T(8,128)(2,1)S(1)} %copy-done, bf16[256,2048]{1,0:T(8,128)(2,1)S(1)} %copy-done.1, ...), custom_call_target="tpu_custom_call" | custom-call | flops 671088640 | bytes 1048576 | tf_op jit(solution)/shard_map/remote_block/pallas_call | solution.py:277
  17.2 3.6 %collective-permute-start.3 = (bf16[512,128]{1,0:T(8,128)(2,1)S(1)}, bf16[512,128]{1,0:T(8,128)(2,1)S(1)}, u32[]{:S(2)}, u32[]{:S(2)}) collective-permute-start(bf16[512,128]{1,0:T(8,128)(2,1)S(1)} %get-tuple-element.37), channel_id=1, source_target_pairs={{0,480},{1,481},{2,482},{3,483},{4,484},{5,485},{6,486},{7,487},{8... | collective-permute-start | bytes 393224 | tf_op jit(solution)/shard_map/ppermute | solution.py:236
  20.8 0.0 collective-permute-done.1.kv_ref.kv2_ref
  20.9 1.3 %remote_block.4 = (bf16[512,128]{1,0:T(8,128)(2,1)S(1)}, bf16[128,2048]{1,0:T(8,128)(2,1)S(1)}, bf16[128,2048]{1,0:T(8,128)(2,1)S(1)}) custom-call(s32[4]{0:T(128)S(4)} %get-tuple-element.22.plan_ref, bf16[256,2048]{1,0:T(8,128)(2,1)S(1)} %copy-done, bf16[256,2048]{1,0:T(8,128)(2,1)S(1)} %copy-done.1, ...), custom_call_target="tpu_custom_call" | custom-call | flops 671088640 | bytes 1048576 | tf_op jit(solution)/shard_map/remote_block/pallas_call | solution.py:277
  22.2 5.6 %collective-permute-start.4 = (bf16[512,128]{1,0:T(8,128)(2,1)S(1)}, bf16[512,128]{1,0:T(8,128)(2,1)S(1)}, u32[]{:S(2)}, u32[]{:S(2)}) collective-permute-start(bf16[512,128]{1,0:T(8,128)(2,1)S(1)} %get-tuple-element.38), channel_id=1, source_target_pairs={{0,31},{1,0},{2,1},{3,2},{4,3},{5,4},{6,5},{7,6},{8,7},{9,8},{10,9... | collective-permute-start | bytes 393224 | tf_op jit(solution)/shard_map/ppermute | solution.py:236
  27.7 0.0 collective-permute-done.2.kv_ref.kv3_ref
  27.7 1.3 %remote_block.5 = (bf16[512,128]{1,0:T(8,128)(2,1)S(1)}, bf16[128,2048]{1,0:T(8,128)(2,1)S(1)}, bf16[128,2048]{1,0:T(8,128)(2,1)S(1)}) custom-call(s32[4]{0:T(128)S(4)} %get-tuple-element.22.plan_ref, bf16[256,2048]{1,0:T(8,128)(2,1)S(1)} %copy-done, bf16[256,2048]{1,0:T(8,128)(2,1)S(1)} %copy-done.1, ...), custom_call_target="tpu_custom_call" | custom-call | flops 671088640 | bytes 1048576 | tf_op jit(solution)/shard_map/remote_block/pallas_call | solution.py:277
  29.1 5.9 %collective-permute-start.5 = (bf16[512,128]{1,0:T(8,128)(2,1)S(1)}, bf16[512,128]{1,0:T(8,128)(2,1)S(1)}, u32[]{:S(2)}, u32[]{:S(2)}) collective-permute-start(bf16[512,128]{1,0:T(8,128)(2,1)S(1)} %get-tuple-element.39), channel_id=1, source_target_pairs={{0,511},{1,480},{2,481},{3,482},{4,483},{5,484},{6,485},{7,486},{8... | collective-permute-start | bytes 393224 | tf_op jit(solution)/shard_map/ppermute | solution.py:236
  35.0 1.9 %last.1 = (bf16[256,2048]{1,0:T(8,128)(2,1)}, bf16[384,2048]{1,0:T(8,128)(2,1)S(1)}, f32[256,128]{1,0:T(8,128)S(1)}, f32[256,128]{1,0:T(8,128)S(1)}) custom-call(s32[4]{0:T(128)S(4)} %get-tuple-element.22.plan_ref, bf16[256,2048]{1,0:T(8,128)(2,1)S(1)} %copy-done, ...), custom_call_target="tpu_custom_call", output_to_operand_aliasing={{1}: (15, {}), {2}: (16, {}), {3}: (17, {})} | custom-call | flops 1342177280 | bytes 1048576 | tf_op jit(solution)/shard_map/last/pallas_call | solution.py:288
  36.9 0.0 collective-permute-done.3
  36.9 0.0 collective-permute-done.4
  36.9 0.0 collective-permute-done.5
  36.9 0.8 %convert_add_fusion = (f32[256,128]{1,0:T(8,128)}, f32[256,128]{1,0:T(8,128)}) fusion(f32[256,128]{1,0:T(8,128)S(1)} %get-tuple-element.40, bf16[512,128]{1,0:T(8,128)(2,1)S(1)} %collective-permute-done.5, bf16[512,128]{1,0:T(8,128)(2,1)S(1)} %collective-permute-done.4, bf16[512,128]{1,0:T(8,128)(2,1)S(1)} %collective-permute-done.3, ...), kind=kLoop, calls=%fused_computation | loop fusion | flops 425984 | bytes 917504 | tf_op jit(solution)/shard_map/add | solution.py:313
Async XLA Ops:
  0.6 12.6 %copy-start = (bf16[256,2048]{1,0:T(8,128)(2,1)S(1)}, bf16[256,2048]{1,0:T(8,128)(2,1)}, u32[]{:S(2)}) copy-start(bf16[256,2048]{1,0:T(8,128)(2,1)} %query_ref.9) | copy-start | bytes 3145732
  0.6 12.6 %copy-start.1 = (bf16[256,2048]{1,0:T(8,128)(2,1)S(1)}, bf16[256,2048]{1,0:T(8,128)(2,1)}, u32[]{:S(2)}) copy-start(bf16[256,2048]{1,0:T(8,128)(2,1)} %grad_ref.9) | copy-start | bytes 3145732
  0.7 12.6 %copy-start.2 = (bf16[256,2048]{1,0:T(8,128)(2,1)S(1)}, bf16[256,2048]{1,0:T(8,128)(2,1)}, u32[]{:S(2)}) copy-start(bf16[256,2048]{1,0:T(8,128)(2,1)} %out_ref.1) | copy-start | bytes 3145732
  0.7 12.6 %copy-start.3 = (f32[16,256]{1,0:T(8,128)S(1)}, f32[16,256]{1,0:T(8,128)}, u32[]{:S(2)}) copy-start(f32[16,256]{1,0:T(8,128)} %sum_ref.1) | copy-start | bytes 49156
  1.7 14.2 %collective-permute-start = (bf16[512,128]{1,0:T(8,128)(2,1)S(1)}, bf16[512,128]{1,0:T(8,128)(2,1)S(1)}, u32[]{:S(2)}, u32[]{:S(2)}) collective-permute-start(bf16[512,128]{1,0:T(8,128)(2,1)S(1)} %get-tuple-element.23.kv_ref), channel_id=1, source_target_pairs={{0,32},{1,33},{2,34},{3,35},{4,36},{5,37},{6,38},{7,39},{8,40},{9,... | collective-permute-start | bytes 393224 | tf_op jit(solution)/shard_map/ppermute | solution.py:236
  5.7 15.2 %collective-permute-start.1 = (bf16[512,128]{1,0:T(8,128)(2,1)S(1)}, bf16[512,128]{1,0:T(8,128)(2,1)S(1)}, u32[]{:S(2)}, u32[]{:S(2)}) collective-permute-start(bf16[512,128]{1,0:T(8,128)(2,1)S(1)} %get-tuple-element.23.kv_ref), channel_id=1, source_target_pairs={{0,1},{1,2},{2,3},{3,4},{4,5},{5,6},{6,7},{7,8},{8,9},{9,10},{10,1... | collective-permute-start | bytes 393224 | tf_op jit(solution)/shard_map/ppermute | solution.py:236
  10.9 16.8 %collective-permute-start.2 = (bf16[512,128]{1,0:T(8,128)(2,1)S(1)}, bf16[512,128]{1,0:T(8,128)(2,1)S(1)}, u32[]{:S(2)}, u32[]{:S(2)}) collective-permute-start(bf16[512,128]{1,0:T(8,128)(2,1)S(1)} %get-tuple-element.23.kv_ref), channel_id=1, source_target_pairs={{0,33},{1,34},{2,35},{3,36},{4,37},{5,38},{6,39},{7,40},{8,41},{9,... | collective-permute-start | bytes 393224 | tf_op jit(solution)/shard_map/ppermute | solution.py:236
  17.2 19.7 %collective-permute-start.3 = (bf16[512,128]{1,0:T(8,128)(2,1)S(1)}, bf16[512,128]{1,0:T(8,128)(2,1)S(1)}, u32[]{:S(2)}, u32[]{:S(2)}) collective-permute-start(bf16[512,128]{1,0:T(8,128)(2,1)S(1)} %get-tuple-element.37), channel_id=1, source_target_pairs={{0,480},{1,481},{2,482},{3,483},{4,484},{5,485},{6,486},{7,487},{8... | collective-permute-start | bytes 393224 | tf_op jit(solution)/shard_map/ppermute | solution.py:236
  22.2 14.8 %collective-permute-start.4 = (bf16[512,128]{1,0:T(8,128)(2,1)S(1)}, bf16[512,128]{1,0:T(8,128)(2,1)S(1)}, u32[]{:S(2)}, u32[]{:S(2)}) collective-permute-start(bf16[512,128]{1,0:T(8,128)(2,1)S(1)} %get-tuple-element.38), channel_id=1, source_target_pairs={{0,31},{1,0},{2,1},{3,2},{4,3},{5,4},{6,5},{7,6},{8,7},{9,8},{10,9... | collective-permute-start | bytes 393224 | tf_op jit(solution)/shard_map/ppermute | solution.py:236
  29.1 7.9 %collective-permute-start.5 = (bf16[512,128]{1,0:T(8,128)(2,1)S(1)}, bf16[512,128]{1,0:T(8,128)(2,1)S(1)}, u32[]{:S(2)}, u32[]{:S(2)}) collective-permute-start(bf16[512,128]{1,0:T(8,128)(2,1)S(1)} %get-tuple-element.39), channel_id=1, source_target_pairs={{0,511},{1,480},{2,481},{3,482},{4,483},{5,484},{6,485},{7,486},{8... | collective-permute-start | bytes 393224 | tf_op jit(solution)/shard_map/ppermute | solution.py:236
